TPU v7x, 256 devices: a whole 4x4x8 slice. The times are simulated.
256 devices in a mesh: member: 16 (over x, z_hi), cell: 16 (over y, z_lo, core).
Axes of the slice: x: 4, y: 4, z: 8 (z_hi: 4, z_lo: 2; z = z_hi * 2 + z_lo), core: 2. Of those that a mesh axis runs over, the one named last changes fastest.
Arguments:
- latent: bfloat16 [16, 24576, 1024], P('member', 'cell'), may hold values from -6 to 6
- w_in: bfloat16 [1024, 1024], replicated, may hold values from -0.1875 to 0.1875
- w_out: bfloat16 [1024, 96], replicated, may hold values from -0.1875 to 0.1875
- target: bfloat16 [96, 24576], P(None, 'cell'), may hold values from -6 to 6
- cell_mask: int32 [24576], P('cell'), may hold values 0 or 1
Outputs:
- grad_w_in: float32 [1024, 1024], P(('member', 'cell'))
- grad_w_out: float32 [1024, 96], P(('member', 'cell'))
All inputs are finite; a program needn't handle non-finite values. No bound on the sum of `cell_mask` on one device may be relied on, other than what follows from the above.
Results may differ from a plain program's by a relative error of at most 0.0055.
Values may be sent and summed in bfloat16 or wider, within the bound.
No kernel may reach another device: no remote copies, remote signals or barrier semaphores. Data moves between devices by JAX's collectives and lax.ppermute only.
A program may use at most 64 MiB of HBM per device.

v0:
```python
import jax
import jax.numpy as jnp
from jax import lax
from jax.sharding import PartitionSpec as P


def in_blocks(x, dim, peers):
    before, after = (x.shape[:dim], x.shape[dim + 1 :])
    return jnp.moveaxis(x.reshape(*before, peers, -1, *after), dim, 0)


def summed_on_arrival(x, axis, dim):
    peers = lax.axis_size(axis)
    tiles = lax.all_to_all(in_blocks(x, dim, peers), axis, 0, 0, tiled=True)
    return jnp.sum(tiles.astype(jnp.float32), axis=0)


def sent_and_summed(x, axis, dim):
    peers = lax.axis_size(axis)
    tiles = lax.all_to_all(in_blocks(x, dim, peers), axis, 0, 0, tiled=True)
    return jnp.sum(tiles, axis=0)


def kernel_fn(diff):
    return diff / jnp.sqrt(1.0 + diff * diff)


def silu_slope(pre):
    gate = jax.nn.sigmoid(pre)
    return gate * (1.0 + pre * (1.0 - gate))


def per_device(latent, w_in, w_out, target, cell_mask):
    members = lax.axis_size("member")
    cell_count = lax.axis_size("cell")
    own_latent = latent[0]
    cells_here = own_latent.shape[0]
    scale = 1.0 / jnp.sqrt(jnp.float32(cells_here * cell_count))
    pre = jnp.dot(own_latent, w_in, preferred_element_type=jnp.float32)
    hidden = jax.nn.silu(pre).astype(jnp.bfloat16)
    fields = lax.dot_general(
        w_out, hidden, (((0,), (1,)), ((), ())), preferred_element_type=jnp.float32
    ).astype(jnp.bfloat16)
    wide = fields.astype(jnp.float32)
    values = lax.all_to_all(fields[None], "member", split_axis=2, concat_axis=0, tiled=True).astype(
        jnp.float32
    )
    sums = jnp.sum(kernel_fn(values[:, None] - values[None, :]), axis=1)
    pair = lax.all_to_all(sums, "member", split_axis=0, concat_axis=2, tiled=True)[0]
    weight = cell_mask.astype(jnp.float32) * scale / members
    own_term = kernel_fn(wide - target.astype(jnp.float32))
    grad_fields = (weight[None] * (own_term - pair / members)).astype(jnp.bfloat16)
    back = lax.dot_general(
        grad_fields, w_out, (((0,), (1,)), ((), ())), preferred_element_type=jnp.float32
    )
    grad_pre = (back * silu_slope(pre)).astype(jnp.bfloat16)
    width = w_in.shape[1]
    grad_in = lax.dot_general(
        own_latent, grad_pre, (((0,), (0,)), ((), ())), preferred_element_type=jnp.float32
    )
    grad_out = lax.dot_general(
        hidden, grad_fields, (((0,), (1,)), ((), ())), preferred_element_type=jnp.float32
    )
    partial_rows = summed_on_arrival(
        jnp.concatenate([grad_in, grad_out], axis=1).astype(jnp.bfloat16), "member", 0
    )
    owned = sent_and_summed(partial_rows, "cell", 0)
    return (owned[:, :width], owned[:, width:])


def solution(mesh):
    in_specs = (P("member", "cell", None), P(), P(), P(None, "cell"), P("cell"))
    out_specs = (P(("member", "cell"), None), P(("member", "cell"), None))
    return jax.shard_map(
        per_device, mesh=mesh, in_specs=in_specs, out_specs=out_specs, check_vma=False
    )
```

profile of v0, /device:TPU:1, one launch (start us, length us, event | category | flops | bytes accessed | tf_op | source)
XLA Modules:
  0.0 188.8 jit_solution(4087096693529205506)
XLA Ops:
  0.6 0.0 copy-start
  0.6 0.0 copy-start.3
  0.7 1.9 copy-done
  2.5 7.5 %multiply_convert_fusion.1 = (bf16[1536,1024]{1,0:T(8,128)(2,1)S(1)}, f32[1536,1024]{1,0:T(8,128)}) fusion(bf16[1024,1024]{1,0:T(8,128)(2,1)} %param.6, bf16[1,1536,1024]{2,1,0:T(8,128)(2,1)S(1)} %copy-done), kind=kOutput, calls=%fused_computation.6 | convolution fusion | flops 3229089792 | bytes 14680064 | tf_op jit(solution)/shard_map/dot_general | solution.py:39
  10.0 0.0 copy-start.1
  10.0 1.7 copy-done.1
  11.7 0.0 copy-done.3
  11.7 1.1 convolution_convert_fusion
  12.8 1.8 copy.23
  14.6 0.5 broadcast.13
  15.1 10.5 %reduce = bf16[1536,96]{1,0:T(8,128)(2,1)} reduce(bf16[1536,1,96]{2,1,0:T(2,128)(2,1)} %bitcast.40, bf16[]{:T(256)} %broadcast.13), dimensions={1}, to_apply=%bitcast.26.reduce_sub_computation | reduce | bytes 589826
  25.7 2.3 %reshape.32 = bf16[16,2,4608]{2,1,0:T(2,128)(2,1)} reshape(bf16[1536,96]{1,0:T(8,128)(2,1)} %reduce) | data formatting | bytes 589824
  27.9 24.5 %all_to_all.28 = bf16[16,2,4608]{2,1,0:T(2,128)(2,1)} all-to-all(bf16[16,2,4608]{2,1,0:T(2,128)(2,1)} %reshape.32), channel_id=1, replica_groups=mesh['member'=16,'cell'=16] {'member'}, dimensions={0} | all-to-all | bytes 589824 | tf_op jit(solution)/shard_map/all_to_all | solution.py:45
  52.5 4.0 %reshape.33 = bf16[1536,1,96]{2,1,0:T(2,128)(2,1)} reshape(bf16[16,2,4608]{2,1,0:T(2,128)(2,1)} %all_to_all.28) | data formatting | bytes 589824
  56.5 0.0 copy-start.4
  56.5 2.6 %bitcast_convert_fusion = f32[1,96,1536]{1,0,2:T(1,128)} fusion(bf16[1536,1,96]{2,1,0:T(2,128)(2,1)} %reshape.33), kind=kLoop, calls=%fused_computation.21 | loop fusion | flops 147456 | bytes 884736 | tf_op jit(solution)/shard_map/sub | solution.py:48
  59.1 2.3 %copy.24 = f32[16,96,96]{2,1,0:T(8,128)} copy(f32[16,96,96]{1,2,0:T(8,128)} %bitcast.39) | data formatting | bytes 1179648 | tf_op jit(solution)/shard_map/sub | solution.py:48
  61.4 5.2 %fusion.2 = f32[16,96,96]{2,1,0:T(8,128)} fusion(f32[16,96,96]{2,1,0:T(8,128)} %copy.24), kind=kLoop, calls=%fused_computation.4 | loop fusion | flops 11649024 | bytes 1179648 | tf_op jit(solution)/shard_map/reduce_sum | solution.py:48
  66.6 4.5 %all-to-all-start.1 = ((f32[16,96,96]{2,1,0:T(8,128)}), f32[16,96,96]{2,1,0:T(8,128)}, u32[]{:S(2)}, u32[]{:S(2)}) async-start(f32[16,96,96]{2,1,0:T(8,128)} %fusion.2), calls=%async_computation.1 | async-start | bytes 1572864 | tf_op jit(solution)/shard_map/all_to_all | solution.py:49
  71.1 0.0 copy-done.4
  71.1 19.8 %all-to-all-done.1 = f32[16,96,96]{2,1,0:T(8,128)} async-done(((f32[16,96,96]{2,1,0:T(8,128)}), f32[16,96,96]{2,1,0:T(8,128)}, u32[]{:S(2)}, u32[]{:S(2)}) %all-to-all-start.1) | async-done | bytes 589856 | tf_op jit(solution)/shard_map/all_to_all | solution.py:49
  90.9 1.2 multiply_bitcast_fusion
  92.1 1.3 copy.26
  93.5 2.3 %div.38 = f32[96,1536]{1,0:T(8,128)} reshape(f32[1,96,16,96]{3,2,1,0:T(8,128)} %copy.26) | data formatting | bytes 1179648 | tf_op jit(solution)/shard_map/div | solution.py:52
  95.7 1.3 multiply_convert_fusion.2
  97.1 0.0 copy-start.2
  97.1 0.7 copy-done.2
  97.8 3.2 %convolution_convert_fusion.1 = bf16[1024,96]{0,1:T(8,128)(2,1)} fusion(bf16[96,1536]{1,0:T(8,128)(2,1)S(1)} %multiply_convert_fusion.2, bf16[1536,1024]{1,0:T(8,128)(2,1)} %copy-done.1), kind=kOutput, calls=%fused_computation.16 | convolution fusion | flops 302088192 | bytes 3637248 | tf_op jit(solution)/shard_map/dot_general | solution.py:61
  101.0 1.1 copy.27
  102.1 7.8 %fusion.7 = bf16[1024,1024]{0,1:T(8,128)(2,1)} fusion(bf16[1,1536,1024]{2,1,0:T(8,128)(2,1)S(1)} %copy-done, f32[1536,1024]{1,0:T(8,128)} %get-tuple-element.3, bf16[96,1536]{1,0:T(8,128)(2,1)} %copy-done.2, bf16[1024,96]{0,1:T(8,128)(2,1)} %param.7), kind=kOutput, calls=%fused_computation.15 | convolution fusion | flops 3538419712 | bytes 12025856 | tf_op jit(solution)/shard_map/dot_general | solution.py:58
  109.9 1.8 pad_maximum_fusion
  111.7 45.2 %all_to_all.29 = bf16[16,64,1120]{2,1,0:T(8,128)(2,1)S(1)} all-to-all(bf16[16,64,1120]{2,1,0:T(8,128)(2,1)S(1)} %pad_maximum_fusion), channel_id=1, replica_groups=mesh['member'=16,'cell'=16] {'member'}, dimensions={0} | all-to-all | bytes 4587520 | tf_op jit(solution)/shard_map/all_to_all | solution.py:14
  156.9 0.3 convert_reduce_fusion
  157.2 0.8 reshape.29
  158.0 29.6 %all_to_all.30 = f32[16,4,1120]{2,1,0:T(4,128)S(1)} all-to-all(f32[16,4,1120]{2,1,0:T(4,128)} %reshape.29), channel_id=1, replica_groups=mesh['member'=16,'cell'=16] {'cell'}, dimensions={0} | all-to-all | bytes 573440 | tf_op jit(solution)/shard_map/all_to_all | solution.py:20
  187.6 0.1 reduce_sum.29
  187.7 0.6 slice.8
  188.3 0.6 slice.9
  (1 shorter events, 0.0 us)
Async XLA Ops:
  0.6 1.9 %copy-start = (bf16[1,1536,1024]{2,1,0:T(8,128)(2,1)S(1)}, bf16[1,1536,1024]{2,1,0:T(8,128)(2,1)}, u32[]{:S(2)}) copy-start(bf16[1,1536,1024]{2,1,0:T(8,128)(2,1)} %param.5) | copy-start | bytes 9437188
  0.6 11.1 %copy-start.3 = (bf16[1024,96]{0,1:T(8,128)(2,1)S(1)}, bf16[1024,96]{0,1:T(8,128)(2,1)}, u32[]{:S(2)}) copy-start(bf16[1024,96]{0,1:T(8,128)(2,1)} %param.7) | copy-start | bytes 589828
  10.0 1.7 copy-start.1
  56.5 14.6 %copy-start.4 = (s32[1536]{0:T(1024)S(1)}, s32[1536]{0:T(1024)}, u32[]{:S(2)}) copy-start(s32[1536]{0:T(1024)} %param.9) | copy-start | bytes 18436
  66.6 24.3 %all-to-all-start.1 = ((f32[16,96,96]{2,1,0:T(8,128)}), f32[16,96,96]{2,1,0:T(8,128)}, u32[]{:S(2)}, u32[]{:S(2)}) async-start(f32[16,96,96]{2,1,0:T(8,128)} %fusion.2), calls=%async_computation.1 | async-start | bytes 1572864 | tf_op jit(solution)/shard_map/all_to_all | solution.py:49
  97.1 0.7 copy-start.2
where the time goes:
time: 190 us; the launch traced here: 189 us
  blocking collectives  99.3 us (52%)
  other arithmetic  23.1 us (12%)
  local copies, waits for them, and re-layouts  21.8 us (11%)
  waiting for transfers between devices  19.8 us (10%)
  matrix products  19.6 us (10%)
  starting transfers between devices  4.46 us (2%)
    all_to_all x1, blocking collectives, summed_on_arrival(): tiles = lax.all_to_all(in_blocks(x, dim, peers), axis, 0, 0, tiled=True)  45.2 us
    all_to_all x1, blocking collectives, sent_and_summed(): tiles = lax.all_to_all(in_blocks(x, dim, peers), axis, 0, 0, tiled=True)  29.6 us
    all_to_all x1, blocking collectives, per_device(): lax.all_to_all(fields[None], 'member', split_axis=2, concat_axis=0, tiled...  24.5 us
    all_to_all x1, waiting for transfers between devices, per_device(): lax.all_to_all(sums, 'member', split_axis=0, concat_axis=2, tiled=True)[0]  19.8 us
    unnamed x13, local copies, waits for them, and re-layouts  11.1 us
    unnamed x1, other arithmetic  10.5 us
    dot_general x1, matrix products, per_device(): lax.dot_general(own_latent, grad_pre, (((0,), (0,)), ((), ())), preferred...  7.77 us
    dot_general x1, matrix products, per_device(): pre = jnp.dot(own_latent, w_in, preferred_element_type=jnp.float32)  7.5 us
  transfers between devices with their start and end apart: 1, of which 1 were waited for; matrix products, arithmetic and copies ran while one was open for 0% of the time, Pallas kernels for 0%

commit v1 on v0

v1 whole, which is shorter than its diff:
```python
import functools

import jax
import jax.numpy as jnp
from jax import lax
from jax.experimental import pallas as pl
from jax.experimental.pallas import tpu as pltpu
from jax.sharding import Mesh, PartitionSpec as P

BF = jnp.bfloat16
F32 = jnp.float32
AXES = ("x", "zh", "y", "zl", "c")
LIMIT = 56 * 1024 * 1024


def params():
    return pltpu.CompilerParams(vmem_limit_bytes=LIMIT)


def mxu(a, b, da, db):
    return lax.dot_general(a, b, (((da,), (db,)), ((), ())), preferred_element_type=F32)


def decode_kernel(groups, latent_ref, w_in_ref, w_out_ref, hidden_ref, slope_ref, fields_ref):
    pre = jnp.dot(latent_ref[0], w_in_ref[...], preferred_element_type=F32)
    gate = 1.0 / (1.0 + jnp.exp(-pre))
    value = pre * gate
    hidden = value.astype(BF)
    hidden_ref[...] = hidden
    slope_ref[...] = (gate + value * (1.0 - gate)).astype(BF)
    fields = mxu(w_out_ref[...], hidden, 1, 1)
    rows = fields.shape[0] // groups
    for g in range(groups):
        fields_ref[g] = fields[g * rows : (g + 1) * rows].astype(BF)


def pair_kernel(scale, fields_ref, target_ref, mask_ref, out_ref, target_rows, value, total):
    members, rows, lanes = fields_ref.shape
    column = pl.multiple_of(lax.axis_index("x") * lanes, 128)
    row = pl.multiple_of(lax.axis_index("zh") * rows, 8)
    target_rows[...] = target_ref[:, pl.ds(column, lanes)].astype(F32)
    target = target_rows[pl.ds(row, rows), :]
    weight = mask_ref[:, pl.ds(column, lanes)].astype(F32) * scale / members
    for m in range(members):
        value[m] = fields_ref[m].astype(F32)
    total[...] = jnp.zeros_like(total)
    for r in range(0, rows, 8):
        for l in range(0, lanes, 128):
            at = (slice(r, r + 8), slice(l, l + 128))
            own = [value[(m,) + at] for m in range(members)]
            sums = [None] * members
            for i in range(members):
                for j in range(i):
                    d = own[i] - own[j]
                    k = d * lax.rsqrt(1.0 + d * d)
                    sums[i] = k if sums[i] is None else sums[i] + k
                    sums[j] = -k if sums[j] is None else sums[j] - k
            for m in range(members):
                total[(m,) + at] = sums[m]
    for m in range(members):
        d = value[m] - target
        k = d * lax.rsqrt(1.0 + d * d)
        out_ref[m] = (weight * (k - total[m] / members)).astype(BF)


def grads_kernel(latent_ref, hidden_ref, slope_ref, fields_ref, w_out_ref, keep_ref, send_ref, acc_in, acc_out):
    step = pl.program_id(0)
    groups, rows, lanes = fields_ref.shape
    grad = fields_ref[...].astype(F32).reshape(groups * rows, lanes).astype(BF)
    back = mxu(grad, w_out_ref[...], 0, 0)
    grad_pre = (back * slope_ref[...].astype(F32)).astype(BF)
    part_in = mxu(latent_ref[0], grad_pre, 0, 0)
    part_out = mxu(hidden_ref[...], grad, 0, 1)
    width = part_out.shape[1]

    @pl.when(step == 0)
    def _():
        acc_in[...] = part_in
        acc_out[...] = jnp.zeros_like(acc_out)
        acc_out[:, :width] = part_out

    @pl.when(step > 0)
    def _():
        acc_in[...] += part_in
        acc_out[:, :width] += part_out

    @pl.when(step == pl.num_programs(0) - 1)
    def _():
        first = lax.axis_index("c") == 0

        def emit(acc, low, high):
            for x in range(4):
                for y in range(4):
                    tiles = []
                    for zh in range(4):
                        at = ((x * 4 + zh) * 4 + y) * 16
                        even, odd = acc[at : at + 8, :], acc[at + 8 : at + 16, :]
                        upper = lax.broadcasted_iota(jnp.int32, even.shape, 0) < 4
                        zero = jnp.where(upper, even, pltpu.roll(odd, 4, 0))
                        one = jnp.where(upper, pltpu.roll(even, 4, 0), odd)
                        tiles.append((zero, one))
                    zero = jnp.concatenate([t[0] for t in tiles], axis=0)
                    one = jnp.concatenate([t[1] for t in tiles], axis=0)
                    keep_ref[x * 4 + y, :, low:high] = jnp.where(first, zero, one).astype(BF)
                    send_ref[x * 4 + y, :, low:high] = jnp.where(first, one, zero).astype(BF)

        emit(acc_in, 0, 1024)
        emit(acc_out, 1024, 1152)


def add_kernel(a_ref, b_ref, out_ref):
    out_ref[...] = (a_ref[...].astype(F32) + b_ref[...].astype(F32)).astype(BF)


def plane_kernel(in_ref, out_ref):
    total = in_ref[0].astype(F32)
    for p in range(1, in_ref.shape[0]):
        total += in_ref[p].astype(F32)
    for z in range(out_ref.shape[0]):
        out_ref[z] = total[4 * z : 4 * z + 4]


def last_kernel(in_ref, grad_in_ref, grad_out_ref):
    total = in_ref[0]
    for z in range(1, in_ref.shape[0]):
        total += in_ref[z]
    width = grad_in_ref.shape[1]
    grad_in_ref[...] = total[:, :width]
    grad_out_ref[...] = total[:, width : width + grad_out_ref.shape[1]]


def per_device(latent, w_in, w_out, target, cell_mask):
    _, cells, depth = latent.shape
    hidden_size, fields_n = w_out.shape
    groups = 4
    block, rows = cells // groups, fields_n // groups
    members = groups * groups
    w_out_t = w_out.T
    total_cells = cells * 16
    scale = 1.0 / float(total_cells) ** 0.5
    whole = lambda *shape: pl.BlockSpec(shape, lambda i: (0,) * len(shape))

    hidden, slope, fields = pl.pallas_call(
        functools.partial(decode_kernel, groups),
        grid=(groups,),
        in_specs=[
            pl.BlockSpec((1, block, depth), lambda i: (0, i, 0)),
            whole(depth, hidden_size),
            whole(fields_n, hidden_size),
        ],
        out_specs=[
            pl.BlockSpec((block, hidden_size), lambda i: (i, 0)),
            pl.BlockSpec((block, hidden_size), lambda i: (i, 0)),
            pl.BlockSpec((groups, rows, block), lambda i: (i, 0, 0)),
        ],
        out_shape=[
            jax.ShapeDtypeStruct((cells, hidden_size), BF),
            jax.ShapeDtypeStruct((cells, hidden_size), BF),
            jax.ShapeDtypeStruct((members, rows, block), BF),
        ],
        compiler_params=params(),
        name="decode",
    )(latent, w_in, w_out_t)

    arrived = lax.all_to_all(fields, ("x", "zh"), 0, 0, tiled=True)

    grads = pl.pallas_call(
        functools.partial(pair_kernel, scale),
        out_shape=jax.ShapeDtypeStruct((members, rows, block), BF),
        scratch_shapes=[
            pltpu.VMEM((fields_n, block), F32),
            pltpu.VMEM((members, rows, block), F32),
            pltpu.VMEM((members, rows, block), F32),
        ],
        compiler_params=params(),
        name="pair",
    )(arrived, target, cell_mask[None])

    grads = lax.all_to_all(grads, ("x", "zh"), 0, 0, tiled=True)

    wide = hidden_size + 128
    half = jax.ShapeDtypeStruct((16, 32, wide), BF)
    keep, send = pl.pallas_call(
        grads_kernel,
        grid=(groups,),
        in_specs=[
            pl.BlockSpec((1, block, depth), lambda i: (0, i, 0)),
            pl.BlockSpec((block, hidden_size), lambda i: (i, 0)),
            pl.BlockSpec((block, hidden_size), lambda i: (i, 0)),
            pl.BlockSpec((groups, rows, block), lambda i: (i, 0, 0)),
            whole(fields_n, hidden_size),
        ],
        out_specs=[whole(16, 32, wide), whole(16, 32, wide)],
        out_shape=[half, half],
        scratch_shapes=[pltpu.VMEM((depth, hidden_size), F32), pltpu.VMEM((depth, 128), F32)],
        compiler_params=params(),
        name="grads",
    )(latent, hidden, slope, grads, w_out_t)

    came = lax.ppermute(send, "c", [(0, 1), (1, 0)])
    both = pl.pallas_call(add_kernel, out_shape=half, compiler_params=params(), name="core_sum")(keep, came)
    plane = lax.all_to_all(both, ("x", "y"), 0, 0, tiled=True)
    line = pl.pallas_call(
        plane_kernel, out_shape=jax.ShapeDtypeStruct((8, 4, wide), F32), compiler_params=params(), name="plane_sum"
    )(plane)
    line = lax.all_to_all(line, ("zh", "zl"), 0, 0, tiled=True)
    return pl.pallas_call(
        last_kernel,
        out_shape=[jax.ShapeDtypeStruct((4, hidden_size), F32), jax.ShapeDtypeStruct((4, fields_n), F32)],
        compiler_params=params(),
        name="line_sum",
    )(line)


def solution(mesh):
    small = Mesh(mesh.devices.reshape(4, 4, 4, 2, 2), AXES)
    member, cell = ("x", "zh"), ("y", "zl", "c")
    in_specs = (P(member, cell, None), P(), P(), P(None, cell), P(cell))
    out_specs = (P(AXES, None), P(AXES, None))
    return jax.shard_map(per_device, mesh=small, in_specs=in_specs, out_specs=out_specs, check_vma=False)
```

time: 190 us -> 115 us (0.61)
  blocking collectives: 99.3 us -> 51.3 us
  Pallas kernels: 0 us -> 31.1 us
  other arithmetic: 23.1 us -> 0 us
  matrix products: 19.6 us -> 0 us
  local copies, waits for them, and re-layouts: 21.8 us -> 2.34 us
  starting transfers between devices: 4.46 us -> 13.9 us
  waiting for transfers between devices: 19.8 us -> 14.9 us
    all_to_all x3, blocking collectives: 99.3 us -> 51.3 us  [the longest x1 22.3 us: per_device(): plane = lax.all_to_all(both, ('x', 'y'), 0, 0, tiled=True)]
    pallas_call x0 -> x6, Pallas kernels: none -> 31.1 us  [the longest x1 12.6 us: per_device(): pl.pallas_call(grads_kernel, grid=(groups,), in_specs=[pl.BlockSpec((1, b...]
    dot_general x4 -> x0, matrix products: 19.6 us -> none  [the longest x1 7.77 us: per_device(): lax.dot_general(own_latent, grad_pre, (((0,), (0,)), ((), ())), preferred...]
    unnamed x1 -> x0, other arithmetic: 10.5 us -> none
    unnamed x13 -> x6, local copies, waits for them, and re-layouts: 11.1 us -> 1.75 us
    all_to_all x1, waiting for transfers between devices: 19.8 us -> 12.2 us  [per_device(): arrived = lax.all_to_all(fields, ('x', 'zh'), 0, 0, tiled=True)]
    all_to_all x1, starting transfers between devices: 4.46 us -> 11.6 us  [per_device(): arrived = lax.all_to_all(fields, ('x', 'zh'), 0, 0, tiled=True)]
    reduce_sum x3 -> x0, other arithmetic: 5.62 us -> none  [the longest x1 5.21 us: per_device(): sums = jnp.sum(kernel_fn(values[:, None] - values[None, :]), axis=1)]
  transfers between devices with their start and end apart: 1 -> 2, of which waited for: 1 -> 2; matrix products, arithmetic and copies ran while one was open for 0% -> 1% of each run, Pallas kernels for 0% -> 0%
where the time goes in v1:
time: 115 us; the launch traced here: 114 us
  blocking collectives  51.3 us (45%)
  Pallas kernels  31.1 us (27%)
  waiting for transfers between devices  14.9 us (13%)
  starting transfers between devices  13.9 us (12%)
  local copies, waits for them, and re-layouts  2.34 us (2%)
    all_to_all x1, blocking collectives, per_device(): plane = lax.all_to_all(both, ('x', 'y'), 0, 0, tiled=True)  22.3 us
    all_to_all x1, blocking collectives, per_device(): grads = lax.all_to_all(grads, ('x', 'zh'), 0, 0, tiled=True)  17 us
    pallas_call x1, Pallas kernels, per_device(): pl.pallas_call(grads_kernel, grid=(groups,), in_specs=[pl.BlockSpec((1, b...  12.6 us
    all_to_all x1, waiting for transfers between devices, per_device(): arrived = lax.all_to_all(fields, ('x', 'zh'), 0, 0, tiled=True)  12.2 us
    all_to_all x1, blocking collectives, per_device(): line = lax.all_to_all(line, ('zh', 'zl'), 0, 0, tiled=True)  12.1 us
    all_to_all x1, starting transfers between devices, per_device(): arrived = lax.all_to_all(fields, ('x', 'zh'), 0, 0, tiled=True)  11.6 us
    pallas_call x1, Pallas kernels, per_device(): pl.pallas_call(functools.partial(decode_kernel, groups), grid=(groups,),...  9 us
    pallas_call x1, Pallas kernels, per_device(): pl.pallas_call(functools.partial(pair_kernel, scale), out_shape=jax.Shape...  2.96 us
  transfers between devices with their start and end apart: 2, of which 2 were waited for; matrix products, arithmetic and copies ran while one was open for 1% of the time, Pallas kernels for 0%

profile of v1, /device:TPU:1, one launch (start us, length us, event | category | flops | bytes accessed | tf_op | source)
XLA Modules:
  0.0 114.2 jit_solution(14742394715257629415)
XLA Ops:
  0.6 0.0 copy-start.2
  0.6 9.0 %decode.1 = (bf16[1536,1024]{1,0:T(8,128)(2,1)}, bf16[1536,1024]{1,0:T(8,128)(2,1)}, bf16[16,24,384]{2,1,0:T(8,128)(2,1)}) custom-call(bf16[1,1536,1024]{2,1,0:T(8,128)(2,1)} %latent_ref.3, bf16[1024,1024]{1,0:T(8,128)(2,1)} %w_in_ref.1, bf16[96,1024]{1,0:T(8,128)(2,1)} %bitcast.1), custom_call_target="tpu_custom_call" | custom-call | tf_op jit(solution)/shard_map/decode/pallas_call | solution.py:143
  9.6 11.6 %all-to-all-start = ((bf16[16,24,384]{2,1,0:T(8,128)(2,1)}), bf16[16,24,384]{2,1,0:T(8,128)(2,1)S(1)}, u32[]{:S(2)}, u32[]{:S(2)}) async-start(bf16[16,24,384]{2,1,0:T(8,128)(2,1)} %get-tuple-element.9), calls=%async_computation | async-start | bytes 589824 | tf_op jit(solution)/shard_map/all_to_all | solution.py:165
  21.2 0.0 copy-done.2
  21.2 0.6 broadcast_in_dim.3.mask_ref
  21.8 12.2 %all-to-all-done.fields_ref = bf16[16,24,384]{2,1,0:T(8,128)(2,1)S(1)} async-done(((bf16[16,24,384]{2,1,0:T(8,128)(2,1)}), bf16[16,24,384]{2,1,0:T(8,128)(2,1)S(1)}, u32[]{:S(2)}, u32[]{:S(2)}) %all-to-all-start) | async-done | bytes 294944 | tf_op jit(solution)/shard_map/all_to_all | solution.py:165
  34.1 0.0 copy-start.1
  34.1 0.7 copy-done.1
  34.8 3.0 %pair.1 = bf16[16,24,384]{2,1,0:T(8,128)(2,1)} custom-call(bf16[16,24,384]{2,1,0:T(8,128)(2,1)} %copy-done.1, bf16[96,1536]{1,0:T(8,128)(2,1)} %target_ref.1, s32[1,1536]{1,0:T(1,128)} %broadcast_in_dim.3.mask_ref), custom_call_target="tpu_custom_call" | custom-call | tf_op jit(solution)/shard_map/pair/pallas_call | solution.py:167
  37.7 17.0 %all_to_all.20.fields_ref = bf16[16,24,384]{2,1,0:T(8,128)(2,1)} all-to-all(bf16[16,24,384]{2,1,0:T(8,128)(2,1)} %pair.1), channel_id=1, replica_groups=mesh['x'=4,'zh'=4,'y'=4,'zl'=2,'c'=2] {'x','zh'}, dimensions={0} | all-to-all | bytes 589824 | tf_op jit(solution)/shard_map/all_to_all | solution.py:179
  54.7 12.6 %grads.1 = (bf16[16,32,1152]{2,1,0:T(8,128)(2,1)}, bf16[16,32,1152]{2,1,0:T(8,128)(2,1)}) custom-call(bf16[1,1536,1024]{2,1,0:T(8,128)(2,1)} %latent_ref.3, bf16[1536,1024]{1,0:T(8,128)(2,1)} %get-tuple-element.7.hidden_ref, bf16[1536,1024]{1,0:T(8,128)(2,1)} %get-tuple-element.8.slope_ref, bf16[16,24,384]{2,1,0:T(8,128)(2,1)} %all_to_all.20.fields_ref, ...), custom_call_target="tpu_custom_call" | custom-call | tf_op jit(solution)/shard_map/grads/pallas_call | solution.py:183
  67.3 2.3 %collective-permute-start = (bf16[16,32,1152]{2,1,0:T(8,128)(2,1)}, bf16[16,32,1152]{2,1,0:T(8,128)(2,1)S(1)}, u32[]{:S(2)}, u32[]{:S(2)}) collective-permute-start(bf16[16,32,1152]{2,1,0:T(8,128)(2,1)} %get-tuple-element.11), channel_id=1, source_target_pairs={{0,1},{1,0},{2,3},{3,2},{4,5},{5,4},{6,7},{7,6},{8,9},{9,8},{10,11... | collective-permute-start | bytes 3538952 | tf_op jit(solution)/shard_map/ppermute | solution.py:200
  69.6 2.7 %collective-permute-done.b_ref = bf16[16,32,1152]{2,1,0:T(8,128)(2,1)S(1)} collective-permute-done((bf16[16,32,1152]{2,1,0:T(8,128)(2,1)}, bf16[16,32,1152]{2,1,0:T(8,128)(2,1)S(1)}, u32[]{:S(2)}, u32[]{:S(2)}) %collective-permute-start) | collective-permute-done | bytes 1179680 | tf_op jit(solution)/shard_map/ppermute | solution.py:200
  72.3 0.0 copy-start
  72.3 1.0 copy-done
  73.3 2.9 %core_sum.1 = bf16[16,32,1152]{2,1,0:T(8,128)(2,1)} custom-call(bf16[16,32,1152]{2,1,0:T(8,128)(2,1)} %get-tuple-element.10.a_ref, bf16[16,32,1152]{2,1,0:T(8,128)(2,1)} %copy-done), custom_call_target="tpu_custom_call" | custom-call | tf_op jit(solution)/shard_map/core_sum/pallas_call | solution.py:201
  76.3 22.3 %all_to_all.21.in_ref = bf16[16,32,1152]{2,1,0:T(8,128)(2,1)} all-to-all(bf16[16,32,1152]{2,1,0:T(8,128)(2,1)} %core_sum.1), channel_id=1, replica_groups=mesh['x'=4,'zh'=4,'y'=4,'zl'=2,'c'=2] {'x','y'}, dimensions={0} | all-to-all | bytes 2359296 | tf_op jit(solution)/shard_map/all_to_all | solution.py:202
  98.5 2.1 %plane_sum.1 = f32[8,4,1152]{2,1,0:T(4,128)} custom-call(bf16[16,32,1152]{2,1,0:T(8,128)(2,1)} %all_to_all.21.in_ref), custom_call_target="tpu_custom_call" | custom-call | tf_op jit(solution)/shard_map/plane_sum/pallas_call | solution.py:203
  100.6 12.1 %all_to_all.22.in_ref = f32[8,4,1152]{2,1,0:T(4,128)} all-to-all(f32[8,4,1152]{2,1,0:T(4,128)} %plane_sum.1), channel_id=1, replica_groups=mesh['x'=4,'zh'=4,'y'=4,'zl'=2,'c'=2] {'zh','zl'}, dimensions={0} | all-to-all | bytes 294912 | tf_op jit(solution)/shard_map/all_to_all | solution.py:206
  112.7 1.5 %line_sum.1 = (f32[4,1024]{1,0:T(4,128)}, f32[4,96]{1,0:T(4,128)}) custom-call(f32[8,4,1152]{2,1,0:T(4,128)} %all_to_all.22.in_ref), custom_call_target="tpu_custom_call" | custom-call | tf_op jit(solution)/shard_map/line_sum/pallas_call | solution.py:207
Async XLA Ops:
  0.6 20.6 %copy-start.2 = (s32[1536]{0:T(1024)S(1)}, s32[1536]{0:T(1024)}, u32[]{:S(2)}) copy-start(s32[1536]{0:T(1024)} %param.9) | copy-start | bytes 18436
  9.6 24.4 %all-to-all-start = ((bf16[16,24,384]{2,1,0:T(8,128)(2,1)}), bf16[16,24,384]{2,1,0:T(8,128)(2,1)S(1)}, u32[]{:S(2)}, u32[]{:S(2)}) async-start(bf16[16,24,384]{2,1,0:T(8,128)(2,1)} %get-tuple-element.9), calls=%async_computation | async-start | bytes 589824 | tf_op jit(solution)/shard_map/all_to_all | solution.py:165
  34.1 0.7 copy-start.1
  67.3 5.0 %collective-permute-start = (bf16[16,32,1152]{2,1,0:T(8,128)(2,1)}, bf16[16,32,1152]{2,1,0:T(8,128)(2,1)S(1)}, u32[]{:S(2)}, u32[]{:S(2)}) collective-permute-start(bf16[16,32,1152]{2,1,0:T(8,128)(2,1)} %get-tuple-element.11), channel_id=1, source_target_pairs={{0,1},{1,0},{2,3},{3,2},{4,5},{5,4},{6,7},{7,6},{8,9},{9,8},{10,11... | collective-permute-start | bytes 3538952 | tf_op jit(solution)/shard_map/ppermute | solution.py:200
  72.3 1.0 copy-start

commit v2 on v1

v2 whole, which is shorter than its diff:
```python
import functools

import jax
import jax.numpy as jnp
from jax import lax
from jax.experimental import pallas as pl
from jax.experimental.pallas import tpu as pltpu
from jax.sharding import Mesh, PartitionSpec as P

BF = jnp.bfloat16
F32 = jnp.float32
AXES = ("x", "zh", "y", "zl", "c")


def params(mib):
    return pltpu.CompilerParams(vmem_limit_bytes=mib * 1024 * 1024)


def mxu(a, b, da, db):
    return lax.dot_general(a, b, (((da,), (db,)), ((), ())), preferred_element_type=F32)


def decode_kernel(
    groups, scale, latent_ref, w_in_ref, w_out_ref, target_ref, mask_ref,
    kept_ref, other_ref, fields_ref, picked_ref, target_rows,
):
    _, rows, lanes = fields_ref.shape
    members = groups * groups

    @pl.when(pl.program_id(0) == 0)
    def _():
        column = pl.multiple_of(lax.axis_index("x") * lanes, 128)
        row = pl.multiple_of(lax.axis_index("zh") * rows, 8)
        target_rows[...] = target_ref[:, pl.ds(column, lanes)].astype(F32)
        picked_ref[:rows] = target_rows[pl.ds(row, rows), :]
        weight = mask_ref[pl.ds(column, lanes)].reshape(1, lanes).astype(F32) * scale / members
        picked_ref[rows:] = jnp.broadcast_to(weight, (8, lanes))

    pre = jnp.dot(latent_ref[0], w_in_ref[...], preferred_element_type=F32)
    gate = 1.0 / (1.0 + jnp.exp(-pre))
    value = pre * gate
    hidden = value.astype(BF)
    kept_ref[:, : hidden.shape[1]] = hidden
    slope = gate + value * (1.0 - gate)
    half = slope.shape[1] // 2
    first = lax.axis_index("c") == 0
    kept_ref[:, hidden.shape[1] :] = jnp.where(first, slope[:, :half], slope[:, half:]).astype(BF)
    other_ref[...] = jnp.where(first, slope[:, half:], slope[:, :half]).astype(BF)
    fields = mxu(w_out_ref[...], hidden, 1, 1)
    for b in range(fields.shape[1] // lanes):
        for g in range(groups):
            fields_ref[b * groups + g] = fields[g * rows : (g + 1) * rows, b * lanes : (b + 1) * lanes].astype(BF)


def pair_kernel(fields_ref, picked_ref, out_ref, value, total):
    members, rows, lanes = fields_ref.shape
    target, weight = picked_ref[:rows], picked_ref[rows : rows + 1]
    for m in range(members):
        value[m] = fields_ref[m].astype(F32)
    for r in range(0, rows, 8):
        for l in range(0, lanes, 128):
            at = (slice(r, r + 8), slice(l, l + 128))
            own = [value[(m,) + at] for m in range(members)]
            sums = [None] * members
            for i in range(members):
                for j in range(i):
                    d = own[i] - own[j]
                    k = d * lax.rsqrt(1.0 + d * d)
                    sums[i] = k if sums[i] is None else sums[i] + k
                    sums[j] = -k if sums[j] is None else sums[j] - k
            for m in range(members):
                total[(m,) + at] = sums[m]
    for m in range(members):
        d = value[m] - target
        k = d * lax.rsqrt(1.0 + d * d)
        out_ref[m] = (weight * (k - total[m] / members)).astype(BF)


def gathered(fields_ref, block, groups):
    _, rows, lanes = fields_ref.shape
    chunks = fields_ref[block * groups : (block + 1) * groups]
    return chunks.astype(F32).reshape(groups * rows, lanes).astype(BF)


def grads_kernel(
    groups, kept_hbm, other_slope_hbm, own_latent_hbm, other_latent_hbm, own_fields_ref, other_fields_ref,
    w_out_ref, sent_hbm, kept, other_slope, own_latent, other_latent, own_pre, other_pre, out_term, sent,
    sems, latent_sems, sent_sems,
):
    lanes, half = own_fields_ref.shape[2], other_slope.shape[1]
    cuts = [slice(b * lanes, (b + 1) * lanes) for b in range(groups)]

    def copies_of(which, source, into):
        return [pltpu.make_async_copy(source.at[cut], into.at[cut], sems.at[which, b]) for b, cut in enumerate(cuts)]

    kepts = copies_of(0, kept_hbm, kept)
    other_slopes = copies_of(1, other_slope_hbm, other_slope)
    latents = [
        pltpu.make_async_copy(own_latent_hbm.at[0], own_latent, latent_sems.at[0]),
        pltpu.make_async_copy(other_latent_hbm.at[0], other_latent, latent_sems.at[1]),
    ]
    for copy in kepts + other_slopes + latents:
        copy.start()

    at = pl.multiple_of(lax.axis_index("c") * half, 128)
    w_out = w_out_ref[:, pl.ds(at, half)]
    fields_n = w_out.shape[0]
    out_term[...] = jnp.zeros_like(out_term)
    for b, cut in enumerate(cuts):
        grad = gathered(own_fields_ref, b, groups)
        back = mxu(grad, w_out, 0, 0)
        kepts[b].wait()
        hidden, slope = kept[cut, : kept.shape[1] - half], kept[cut, kept.shape[1] - half :]
        own_pre[cut] = (back * slope.astype(F32)).astype(BF)
        out_term[:fields_n] += jnp.dot(grad, hidden, preferred_element_type=F32)
    for b, cut in enumerate(cuts):
        back = mxu(gathered(other_fields_ref, b, groups), w_out, 0, 0)
        other_slopes[b].wait()
        other_pre[cut] = (back * other_slope[cut].astype(F32)).astype(BF)

    for copy in latents:
        copy.wait()
    chunks, chunk_rows, _ = sent.shape
    xs = ys = groups
    quarter = own_latent.shape[1] // xs
    outs = []
    for x in range(xs):
        of_x = slice(x * quarter, (x + 1) * quarter)
        total = mxu(own_latent[:, of_x], own_pre[...], 0, 0) + mxu(other_latent[:, of_x], other_pre[...], 0, 0)
        total = total.astype(BF)
        term = out_term[:, of_x].T.astype(BF)
        for y in range(ys):
            for zh in range(chunk_rows // 16):
                rows = slice((zh * ys + y) * 16, (zh * ys + y + 1) * 16)
                into = slice(zh * 16, (zh + 1) * 16)
                sent[x * ys + y, into, :half] = total[rows]
                sent[x * ys + y, into, half:] = term[rows]
        part = pl.ds(x * ys, ys)
        outs.append(pltpu.make_async_copy(sent.at[part], sent_hbm.at[part], sent_sems.at[x]))
        outs[-1].start()
    for copy in outs:
        copy.wait()


def plane_kernel(in_ref, out_ref):
    total = in_ref[0].astype(F32)
    for p in range(1, in_ref.shape[0]):
        total += in_ref[p].astype(F32)
    rows = out_ref.shape[1]
    for z in range(out_ref.shape[0]):
        out_ref[z] = total[rows * z : rows * (z + 1)]


def last_kernel(in_ref, grad_in_ref, grad_out_ref):
    first, second = in_ref[0], in_ref[1]
    for z in range(2, in_ref.shape[0], 2):
        first += in_ref[z]
        second += in_ref[z + 1]
    half = grad_in_ref.shape[1] // 2
    grad_in_ref[:, :half] = first[:, :half]
    grad_in_ref[:, half:] = second[:, :half]
    grad_out_ref[...] = (first + second)[:, half : half + grad_out_ref.shape[1]]


def shape(*dims, dtype=BF):
    return jax.ShapeDtypeStruct(dims, dtype)


def per_device(latent, w_in, w_out, target, cell_mask):
    _, cells, depth = latent.shape
    hidden_size, fields_n = w_out.shape
    groups = 4
    block, rows = cells // groups, fields_n // groups
    members = groups * groups
    half = hidden_size // 2
    wide = half + 128
    w_out_t = w_out.T
    scale = 1.0 / float(cells * 16) ** 0.5
    whole = lambda *shape: pl.BlockSpec(shape, lambda i, *_: (0,) * len(shape))
    swap = [(0, 1), (1, 0)]
    hbm = pl.BlockSpec(memory_space=pltpu.HBM)
    vmem = pl.BlockSpec(memory_space=pltpu.VMEM)
    step = 2 * block
    halves = pl.BlockSpec((step, half), lambda i: (i, 0))

    kept, other_slope, fields, picked = pl.pallas_call(
        functools.partial(decode_kernel, groups, scale),
        grid=(cells // step,),
        in_specs=[
            pl.BlockSpec((1, step, depth), lambda i: (0, i, 0)),
            whole(depth, hidden_size),
            whole(fields_n, hidden_size),
            whole(fields_n, cells),
            whole(cells),
        ],
        out_specs=[
            pl.BlockSpec((step, hidden_size + half), lambda i: (i, 0)),
            halves,
            pl.BlockSpec((2 * groups, rows, block), lambda i: (i, 0, 0)),
            whole(rows + 8, block),
        ],
        out_shape=[
            shape(cells, hidden_size + half),
            shape(cells, half),
            shape(members, rows, block),
            shape(rows + 8, block, dtype=F32),
        ],
        scratch_shapes=[pltpu.VMEM((fields_n, block), F32)],
        compiler_params=params(58),
        name="decode",
    )(latent, w_in, w_out_t, target, cell_mask)

    arrived = lax.all_to_all(fields, ("x", "zh"), 0, 0, tiled=True)
    other_slope = lax.ppermute(other_slope, "c", swap)
    other_latent = lax.ppermute(latent, "c", swap)

    grads = pl.pallas_call(
        pair_kernel,
        out_shape=shape(members, rows, block),
        scratch_shapes=[pltpu.VMEM((members, rows, block), F32), pltpu.VMEM((members, rows, block), F32)],
        compiler_params=params(16),
        name="pair",
    )(arrived, picked)

    grads = lax.all_to_all(grads, ("x", "zh"), 0, 0, tiled=True)
    other_grads = lax.ppermute(grads, "c", swap)

    xs, ys, zs = 4, 4, 8
    chunks = (xs * ys, depth // (xs * ys), wide)
    terms = pl.pallas_call(
        functools.partial(grads_kernel, groups),
        in_specs=[hbm] * 4 + [vmem] * 3,
        out_specs=hbm,
        out_shape=shape(*chunks),
        scratch_shapes=[
            pltpu.VMEM((cells, hidden_size + half), BF),
            pltpu.VMEM((cells, half), BF),
            pltpu.VMEM((cells, depth), BF),
            pltpu.VMEM((cells, depth), BF),
            pltpu.VMEM((cells, half), BF),
            pltpu.VMEM((cells, half), BF),
            pltpu.VMEM((128, hidden_size), F32),
            pltpu.VMEM(chunks, BF),
            pltpu.SemaphoreType.DMA((2, groups)),
            pltpu.SemaphoreType.DMA((2,)),
            pltpu.SemaphoreType.DMA((xs,)),
        ],
        compiler_params=params(43),
        name="weight_grads",
    )(kept, other_slope, latent, other_latent, grads, other_grads, w_out_t)

    plane = lax.all_to_all(terms, ("x", "y"), 0, 0, tiled=True)
    line = pl.pallas_call(
        plane_kernel,
        out_shape=shape(2 * zs, 4, wide, dtype=F32),
        compiler_params=params(16),
        name="plane_sum",
    )(plane)
    line = lax.all_to_all(line, ("zh", "zl", "c"), 0, 0, tiled=True)
    return pl.pallas_call(
        last_kernel,
        out_shape=[shape(4, hidden_size, dtype=F32), shape(4, fields_n, dtype=F32)],
        compiler_params=params(16),
        name="line_sum",
    )(line)


def solution(mesh):
    small = Mesh(mesh.devices.reshape(4, 4, 4, 2, 2), AXES)
    member, cell = ("x", "zh"), ("y", "zl", "c")
    in_specs = (P(member, cell, None), P(), P(), P(None, cell), P(cell))
    out_specs = (P(AXES, None), P(AXES, None))
    return jax.shard_map(per_device, mesh=small, in_specs=in_specs, out_specs=out_specs, check_vma=False)
```

time: 115 us -> 103 us (0.90)
  blocking collectives: 51.3 us -> 74.8 us
  waiting for transfers between devices: 14.9 us -> 1.21 us
  Pallas kernels: 31.1 us -> 19.8 us
  starting transfers between devices: 13.9 us -> 5.71 us
  local copies, waits for them, and re-layouts: 2.34 us -> 0.81 us
    all_to_all x2 -> x3, blocking collectives: 34.4 us -> 59.2 us  [the longest x1 23.2 us: per_device(): plane = lax.all_to_all(terms, ('x', 'y'), 0, 0, tiled=True)]
    all_to_all x1 -> x0, waiting for transfers between devices: 12.2 us -> none  [per_device(): arrived = lax.all_to_all(fields, ('x', 'zh'), 0, 0, tiled=True)]
    all_to_all x1 -> x0, starting transfers between devices: 11.6 us -> none  [per_device(): arrived = lax.all_to_all(fields, ('x', 'zh'), 0, 0, tiled=True)]
    pallas_call x6 -> x5, Pallas kernels: 31.1 us -> 19.8 us  [the longest x1 8.97 us: per_device(): pl.pallas_call(functools.partial(grads_kernel, groups), in_specs=[hbm] *...]
    ppermute x1 -> x3, starting transfers between devices: 2.29 us -> 5.71 us  [the longest x1 3.33 us: per_device(): other_latent = lax.ppermute(latent, 'c', swap)]
    ppermute x1 -> x3, waiting for transfers between devices: 2.68 us -> 1.21 us  [the longest x1 1.21 us: per_device(): other_grads = lax.ppermute(grads, 'c', swap)]
    all_to_all x1, blocking collectives: 17 us -> 15.6 us  [per_device(): grads = lax.all_to_all(grads, ('x', 'zh'), 0, 0, tiled=True)]
  transfers between devices with their start and end apart: 2 -> 3, of which waited for: 2 -> 1; matrix products, arithmetic and copies ran while one was open for 1% -> 0% of each run, Pallas kernels for 0% -> 10%
where the time goes in v2:
time: 103 us
  blocking collectives  74.8 us (73%)
  Pallas kernels  19.8 us (19%)
  starting transfers between devices  5.71 us (6%)
  waiting for transfers between devices  1.21 us (1%)
    all_to_all x1, blocking collectives, per_device(): plane = lax.all_to_all(terms, ('x', 'y'), 0, 0, tiled=True)  23.2 us
    all_to_all x1, blocking collectives, per_device(): arrived = lax.all_to_all(fields, ('x', 'zh'), 0, 0, tiled=True)  21.9 us
    all_to_all x1, blocking collectives, per_device(): grads = lax.all_to_all(grads, ('x', 'zh'), 0, 0, tiled=True)  15.6 us
    all_to_all x1, blocking collectives, per_device(): line = lax.all_to_all(line, ('zh', 'zl', 'c'), 0, 0, tiled=True)  14.1 us
    pallas_call x1, Pallas kernels, per_device(): pl.pallas_call(functools.partial(grads_kernel, groups), in_specs=[hbm] *...  8.97 us
    pallas_call x1, Pallas kernels, per_device(): pl.pallas_call(functools.partial(decode_kernel, groups, scale), grid=(cel...  8.9 us
    ppermute x1, starting transfers between devices, per_device(): other_latent = lax.ppermute(latent, 'c', swap)  3.33 us
    ppermute x1, starting transfers between devices, per_device(): other_grads = lax.ppermute(grads, 'c', swap)  2.27 us
  transfers between devices with their start and end apart: 3, of which 1 were waited for; matrix products, arithmetic and copies ran while one was open for 0% of the time, Pallas kernels for 10%

profile of v2, /device:TPU:1, one launch (start us, length us, event | category | flops | bytes accessed | tf_op | source)
XLA Modules:
  0.0 103.0 jit_solution(6023524473539005329)
XLA Ops:
  0.6 3.3 %collective-permute-start.1 = (bf16[1,1536,1024]{2,1,0:T(8,128)(2,1)}, bf16[1,1536,1024]{2,1,0:T(8,128)(2,1)}, u32[]{:S(2)}, u32[]{:S(2)}) collective-permute-start(bf16[1,1536,1024]{2,1,0:T(8,128)(2,1)} %own_latent_hbm.1), channel_id=1, source_target_pairs={{0,1},{1,0},{2,3},{3,2},{4,5},{5,4},{6,7},{7,6},{8,9},{9,8},{10,11... | collective-permute-start | bytes 9437192 | tf_op jit(solution)/shard_map/ppermute | solution.py:215
  4.0 0.0 copy-start
  4.0 0.0 copy-start.1
  4.0 8.9 %decode.1 = (bf16[1536,1536]{1,0:T(8,128)(2,1)}, bf16[1536,512]{1,0:T(8,128)(2,1)}, bf16[16,24,384]{2,1,0:T(8,128)(2,1)}, f32[32,384]{1,0:T(8,128)}) custom-call(bf16[1,1536,1024]{2,1,0:T(8,128)(2,1)} %own_latent_hbm.1, bf16[1024,1024]{1,0:T(8,128)(2,1)} %w_in_ref.1, bf16[96,1024]{1,0:T(8,128)(2,1)} %bitcast.1, bf16[96,1536]{1,0:T(8,128)(2,1)} %target_ref.1, ...), custom_call_target="tpu_custom_call" | custom-call | tf_op jit(solution)/shard_map/decode/pallas_call | solution.py:186
  12.9 0.1 collective-permute-start
  13.0 21.9 %all_to_all.20.fields_ref = bf16[16,24,384]{2,1,0:T(8,128)(2,1)S(1)} all-to-all(bf16[16,24,384]{2,1,0:T(8,128)(2,1)} %get-tuple-element.8), channel_id=1, replica_groups=mesh['x'=4,'zh'=4,'y'=4,'zl'=2,'c'=2] {'x','zh'}, dimensions={0} | all-to-all | bytes 589824 | tf_op jit(solution)/shard_map/all_to_all | solution.py:213
  34.9 0.0 copy-start.2
  34.9 0.8 copy-done.2
  35.7 1.2 %pair.1 = bf16[16,24,384]{2,1,0:T(8,128)(2,1)S(1)} custom-call(bf16[16,24,384]{2,1,0:T(8,128)(2,1)S(1)} %all_to_all.20.fields_ref, f32[32,384]{1,0:T(8,128)S(1)} %copy-done.2), custom_call_target="tpu_custom_call" | custom-call | tf_op jit(solution)/shard_map/pair/pallas_call | solution.py:217
  36.9 15.6 %all_to_all.21.own_fields_ref = bf16[16,24,384]{2,1,0:T(8,128)(2,1)S(1)} all-to-all(bf16[16,24,384]{2,1,0:T(8,128)(2,1)S(1)} %pair.1), channel_id=1, replica_groups=mesh['x'=4,'zh'=4,'y'=4,'zl'=2,'c'=2] {'x','zh'}, dimensions={0} | all-to-all | bytes 589824 | tf_op jit(solution)/shard_map/all_to_all | solution.py:225
  52.5 2.3 %collective-permute-start.2 = (bf16[16,24,384]{2,1,0:T(8,128)(2,1)S(1)}, bf16[16,24,384]{2,1,0:T(8,128)(2,1)S(1)}, u32[]{:S(2)}, u32[]{:S(2)}) collective-permute-start(bf16[16,24,384]{2,1,0:T(8,128)(2,1)S(1)} %all_to_all.21.own_fields_ref), channel_id=1, source_target_pairs={{0,1},{1,0},{2,3},{3,2},{4,5},{5,4},{6,7},{7,6},{8,9},{9,8},{10,11... | collective-permute-start | bytes 884744 | tf_op jit(solution)/shard_map/ppermute | solution.py:226
  54.8 1.2 %collective-permute-done.2.other_fields_ref = bf16[16,24,384]{2,1,0:T(8,128)(2,1)S(1)} collective-permute-done((bf16[16,24,384]{2,1,0:T(8,128)(2,1)S(1)}, bf16[16,24,384]{2,1,0:T(8,128)(2,1)S(1)}, u32[]{:S(2)}, u32[]{:S(2)}) %collective-permute-start.2) | collective-permute-done | bytes 294944 | tf_op jit(solution)/shard_map/ppermute | solution.py:226
  56.0 0.0 collective-permute-done.other_slope_hbm
  56.0 0.0 collective-permute-done.1.other_latent_hbm
  56.0 0.0 copy-done
  56.0 0.0 copy-done.1
  56.0 9.0 %weight_grads.1 = bf16[16,64,640]{2,1,0:T(8,128)(2,1)S(1)} custom-call(bf16[1536,1536]{1,0:T(8,128)(2,1)} %get-tuple-element.6.kept_hbm, bf16[1536,512]{1,0:T(8,128)(2,1)S(1)} %collective-permute-done.other_slope_hbm, bf16[1,1536,1024]{2,1,0:T(8,128)(2,1)S(1)} %copy-done, bf16[1,1536,1024]{2,1,0:T(8,128)(2,1)} %collective-permute-done.1.other_latent_hbm, ...), custom_call_target="tpu_custom_call" | custom-call | tf_op jit(solution)/shard_map/weight_grads/pallas_call | solution.py:230
  65.0 23.2 %all_to_all.22.in_ref = bf16[16,64,640]{2,1,0:T(8,128)(2,1)S(1)} all-to-all(bf16[16,64,640]{2,1,0:T(8,128)(2,1)S(1)} %weight_grads.1), channel_id=1, replica_groups=mesh['x'=4,'zh'=4,'y'=4,'zl'=2,'c'=2] {'x','y'}, dimensions={0} | all-to-all | bytes 2621440 | tf_op jit(solution)/shard_map/all_to_all | solution.py:252
  88.1 0.2 plane_sum.1
  88.3 14.1 %all_to_all.23.in_ref = f32[16,4,640]{2,1,0:T(4,128)S(1)} all-to-all(f32[16,4,640]{2,1,0:T(4,128)S(1)} %plane_sum.1), channel_id=1, replica_groups=mesh['x'=4,'zh'=4,'y'=4,'zl'=2,'c'=2] {'zh','zl','c'}, dimensions={0} | all-to-all | bytes 327680 | tf_op jit(solution)/shard_map/all_to_all | solution.py:259
  102.4 0.6 line_sum.1
Async XLA Ops:
  0.6 55.3 %collective-permute-start.1 = (bf16[1,1536,1024]{2,1,0:T(8,128)(2,1)}, bf16[1,1536,1024]{2,1,0:T(8,128)(2,1)}, u32[]{:S(2)}, u32[]{:S(2)}) collective-permute-start(bf16[1,1536,1024]{2,1,0:T(8,128)(2,1)} %own_latent_hbm.1), channel_id=1, source_target_pairs={{0,1},{1,0},{2,3},{3,2},{4,5},{5,4},{6,7},{7,6},{8,9},{9,8},{10,11... | collective-permute-start | bytes 9437192 | tf_op jit(solution)/shard_map/ppermute | solution.py:215
  4.0 52.0 %copy-start = (bf16[1,1536,1024]{2,1,0:T(8,128)(2,1)S(1)}, bf16[1,1536,1024]{2,1,0:T(8,128)(2,1)}, u32[]{:S(2)}) copy-start(bf16[1,1536,1024]{2,1,0:T(8,128)(2,1)} %own_latent_hbm.1) | copy-start | bytes 9437188
  4.0 52.0 %copy-start.1 = (bf16[1024,96]{0,1:T(8,128)(2,1)S(1)}, bf16[1024,96]{0,1:T(8,128)(2,1)}, u32[]{:S(2)}) copy-start(bf16[1024,96]{0,1:T(8,128)(2,1)} %param.7) | copy-start | bytes 589828
  12.9 43.1 %collective-permute-start = (bf16[1536,512]{1,0:T(8,128)(2,1)}, bf16[1536,512]{1,0:T(8,128)(2,1)S(1)}, u32[]{:S(2)}, u32[]{:S(2)}) collective-permute-start(bf16[1536,512]{1,0:T(8,128)(2,1)} %get-tuple-element.7), channel_id=1, source_target_pairs={{0,1},{1,0},{2,3},{3,2},{4,5},{5,4},{6,7},{7,6},{8,9},{9,8},{10,11... | collective-permute-start | bytes 4718600 | tf_op jit(solution)/shard_map/ppermute | solution.py:214
  34.9 0.8 copy-start.2
  52.5 3.5 %collective-permute-start.2 = (bf16[16,24,384]{2,1,0:T(8,128)(2,1)S(1)}, bf16[16,24,384]{2,1,0:T(8,128)(2,1)S(1)}, u32[]{:S(2)}, u32[]{:S(2)}) collective-permute-start(bf16[16,24,384]{2,1,0:T(8,128)(2,1)S(1)} %all_to_all.21.own_fields_ref), channel_id=1, source_target_pairs={{0,1},{1,0},{2,3},{3,2},{4,5},{5,4},{6,7},{7,6},{8,9},{9,8},{10,11... | collective-permute-start | bytes 884744 | tf_op jit(solution)/shard_map/ppermute | solution.py:226

commit v3 on v2

--- a/solution.py
+++ b/solution.py
@@ -82,10 +82,30 @@
     return chunks.astype(F32).reshape(groups * rows, lanes).astype(BF)
 
 
+class Rows:
+    def __init__(self, k, own_hbm, other_hbm, own, other, sems):
+        quarter = own.shape[1]
+        to = lax.rem(lax.axis_index("x") + k, 4)
+        self.at = pl.ds(pl.multiple_of(to * quarter, 128), quarter)
+        self.own, self.other = own, other
+        self.own_copy = pltpu.make_async_copy(own_hbm.at[0, :, self.at], own, sems.at[0])
+        self.other_copy = pltpu.make_async_copy(other_hbm.at[0, :, self.at], other, sems.at[1])
+
+    def start(self):
+        self.own_copy.start()
+        self.other_copy.start()
+
+    def value(self, own_pre, other_pre, out_term):
+        self.own_copy.wait()
+        self.other_copy.wait()
+        total = mxu(self.own[...], own_pre[...], 0, 0) + mxu(self.other[...], other_pre[...], 0, 0)
+        return jnp.concatenate([total, out_term[:, self.at].T], axis=1)
+
+
 def grads_kernel(
     groups, kept_hbm, other_slope_hbm, own_latent_hbm, other_latent_hbm, own_fields_ref, other_fields_ref,
-    w_out_ref, sent_hbm, kept, other_slope, own_latent, other_latent, own_pre, other_pre, out_term, sent,
-    sems, latent_sems, sent_sems,
+    w_out_ref, own_pre, other_pre, out_term, top_ref, bottom_ref, kept, other_slope, own_latent, other_latent,
+    sems, latent_sems,
 ):
     lanes, half = own_fields_ref.shape[2], other_slope.shape[1]
     cuts = [slice(b * lanes, (b + 1) * lanes) for b in range(groups)]
@@ -95,12 +115,10 @@
 
     kepts = copies_of(0, kept_hbm, kept)
     other_slopes = copies_of(1, other_slope_hbm, other_slope)
-    latents = [
-        pltpu.make_async_copy(own_latent_hbm.at[0], own_latent, latent_sems.at[0]),
-        pltpu.make_async_copy(other_latent_hbm.at[0], other_latent, latent_sems.at[1]),
-    ]
-    for copy in kepts + other_slopes + latents:
+    latents = Rows(2, own_latent_hbm, other_latent_hbm, own_latent, other_latent, latent_sems)
+    for copy in kepts + other_slopes:
         copy.start()
+    latents.start()
 
     at = pl.multiple_of(lax.axis_index("c") * half, 128)
     w_out = w_out_ref[:, pl.ds(at, half)]
@@ -118,44 +136,42 @@
         other_slopes[b].wait()
         other_pre[cut] = (back * other_slope[cut].astype(F32)).astype(BF)
 
-    for copy in latents:
-        copy.wait()
-    chunks, chunk_rows, _ = sent.shape
-    xs = ys = groups
-    quarter = own_latent.shape[1] // xs
-    outs = []
-    for x in range(xs):
-        of_x = slice(x * quarter, (x + 1) * quarter)
-        total = mxu(own_latent[:, of_x], own_pre[...], 0, 0) + mxu(other_latent[:, of_x], other_pre[...], 0, 0)
-        total = total.astype(BF)
-        term = out_term[:, of_x].T.astype(BF)
-        for y in range(ys):
-            for zh in range(chunk_rows // 16):
-                rows = slice((zh * ys + y) * 16, (zh * ys + y + 1) * 16)
-                into = slice(zh * 16, (zh + 1) * 16)
-                sent[x * ys + y, into, :half] = total[rows]
-                sent[x * ys + y, into, half:] = term[rows]
-        part = pl.ds(x * ys, ys)
-        outs.append(pltpu.make_async_copy(sent.at[part], sent_hbm.at[part], sent_sems.at[x]))
-        outs[-1].start()
-    for copy in outs:
-        copy.wait()
-
-
-def plane_kernel(in_ref, out_ref):
-    total = in_ref[0].astype(F32)
-    for p in range(1, in_ref.shape[0]):
-        total += in_ref[p].astype(F32)
+    total = latents.value(own_pre, other_pre, out_term)
+    middle = top_ref.shape[0]
+    top_ref[...] = total[:middle].astype(BF)
+    bottom_ref[...] = total[middle:].astype(BF)
+
+
+def rest_kernel(own_latent_hbm, other_latent_hbm, own_pre, other_pre, out_term, on_ref, back_ref, stay_ref, own_latent, other_latent, sems):
+    parts = []
+    for i, (k, ref) in enumerate(((1, on_ref), (3, back_ref), (0, stay_ref))):
+        rows = Rows(k, own_latent_hbm, other_latent_hbm, own_latent.at[i], other_latent.at[i], sems.at[i])
+        rows.start()
+        parts.append((rows, ref))
+    for rows, ref in parts:
+        ref[...] = rows.value(own_pre, other_pre, out_term)
+
+
+def pass_kernel(on_ref, back_ref, top_ref, bottom_ref, on_out, back_out):
+    middle = top_ref.shape[0]
+    on_out[:middle] = (on_ref[:middle] + top_ref[...].astype(F32)).astype(BF)
+    on_out[middle:] = on_ref[middle:].astype(BF)
+    back_out[:middle] = back_ref[:middle].astype(BF)
+    back_out[middle:] = (back_ref[middle:] + bottom_ref[...].astype(F32)).astype(BF)
+
+
+def x_kernel(stay_ref, on_ref, back_ref, out_ref):
+    total = stay_ref[...] + on_ref[...].astype(F32) + back_ref[...].astype(F32)
     rows = out_ref.shape[1]
-    for z in range(out_ref.shape[0]):
-        out_ref[z] = total[rows * z : rows * (z + 1)]
+    for p in range(out_ref.shape[0]):
+        out_ref[p] = total[rows * p : rows * (p + 1)].astype(BF)
 
 
 def last_kernel(in_ref, grad_in_ref, grad_out_ref):
-    first, second = in_ref[0], in_ref[1]
+    first, second = in_ref[0].astype(F32), in_ref[1].astype(F32)
     for z in range(2, in_ref.shape[0], 2):
-        first += in_ref[z]
-        second += in_ref[z + 1]
+        first += in_ref[z].astype(F32)
+        second += in_ref[z + 1].astype(F32)
     half = grad_in_ref.shape[1] // 2
     grad_in_ref[:, :half] = first[:, :half]
     grad_in_ref[:, half:] = second[:, :half]
@@ -225,38 +241,53 @@
     grads = lax.all_to_all(grads, ("x", "zh"), 0, 0, tiled=True)
     other_grads = lax.ppermute(grads, "c", swap)
 
-    xs, ys, zs = 4, 4, 8
-    chunks = (xs * ys, depth // (xs * ys), wide)
-    terms = pl.pallas_call(
+    quarter = depth // 4
+    own_pre, other_pre, out_term, top, bottom = pl.pallas_call(
         functools.partial(grads_kernel, groups),
         in_specs=[hbm] * 4 + [vmem] * 3,
-        out_specs=hbm,
-        out_shape=shape(*chunks),
+        out_shape=[
+            shape(cells, half),
+            shape(cells, half),
+            shape(128, hidden_size, dtype=F32),
+            shape(quarter // 2, wide),
+            shape(quarter // 2, wide),
+        ],
         scratch_shapes=[
             pltpu.VMEM((cells, hidden_size + half), BF),
             pltpu.VMEM((cells, half), BF),
-            pltpu.VMEM((cells, depth), BF),
-            pltpu.VMEM((cells, depth), BF),
-            pltpu.VMEM((cells, half), BF),
-            pltpu.VMEM((cells, half), BF),
-            pltpu.VMEM((128, hidden_size), F32),
-            pltpu.VMEM(chunks, BF),
+            pltpu.VMEM((cells, quarter), BF),
+            pltpu.VMEM((cells, quarter), BF),
             pltpu.SemaphoreType.DMA((2, groups)),
             pltpu.SemaphoreType.DMA((2,)),
-            pltpu.SemaphoreType.DMA((xs,)),
-        ],
-        compiler_params=params(43),
+        ],
+        compiler_params=params(40),
+        name="grad_pre",
+    )(kept, other_slope, latent, other_latent, grads, other_grads, w_out_t)
+
+    right = [(i, (i + 1) % 4) for i in range(4)]
+    left = [(i, (i + 3) % 4) for i in range(4)]
+    top, bottom = lax.ppermute(top, "x", right), lax.ppermute(bottom, "x", left)
+    on, back, stay = pl.pallas_call(
+        rest_kernel,
+        in_specs=[hbm] * 2 + [vmem] * 3,
+        out_shape=[shape(quarter, wide, dtype=F32)] * 3,
+        scratch_shapes=[
+            pltpu.VMEM((3, cells, quarter), BF),
+            pltpu.VMEM((3, cells, quarter), BF),
+            pltpu.SemaphoreType.DMA((3, 2)),
+        ],
+        compiler_params=params(24),
+        cost_estimate=pl.CostEstimate(flops=12 * quarter * cells * half, bytes_accessed=12 << 20, transcendentals=0),
         name="weight_grads",
-    )(kept, other_slope, latent, other_latent, grads, other_grads, w_out_t)
-
-    plane = lax.all_to_all(terms, ("x", "y"), 0, 0, tiled=True)
+    )(latent, other_latent, own_pre, other_pre, out_term)
+    on, back = pl.pallas_call(
+        pass_kernel, out_shape=[shape(quarter, wide)] * 2, compiler_params=params(16), name="pass_on"
+    )(on, back, top, bottom)
+    on, back = lax.ppermute(on, "x", right), lax.ppermute(back, "x", left)
     line = pl.pallas_call(
-        plane_kernel,
-        out_shape=shape(2 * zs, 4, wide, dtype=F32),
-        compiler_params=params(16),
-        name="plane_sum",
-    )(plane)
-    line = lax.all_to_all(line, ("zh", "zl", "c"), 0, 0, tiled=True)
+        x_kernel, out_shape=shape(64, 4, wide), compiler_params=params(16), name="x_sum"
+    )(stay, on, back)
+    line = lax.all_to_all(line, ("zh", "y", "zl", "c"), 0, 0, tiled=True)
     return pl.pallas_call(
         last_kernel,
         out_shape=[shape(4, hidden_size, dtype=F32), shape(4, fields_n, dtype=F32)],

time: 103 us -> 99.8 us (0.969)
  blocking collectives: 74.8 us -> 58 us
  waiting for transfers between devices: 1.21 us -> 8.05 us
  starting transfers between devices: 5.71 us -> 11.1 us
    all_to_all x2 -> x1, blocking collectives: 37.3 us -> 20.5 us  [per_device(): line = lax.all_to_all(line, ('zh', 'y', 'zl', 'c'), 0, 0, tiled=True)]
    ppermute x0 -> x4, waiting for transfers between devices: none -> 6.83 us  [the longest x2 6.83 us: per_device(): on, back = (lax.ppermute(on, 'x', right), lax.ppermute(back, 'x', left))]
    ppermute x0 -> x4, starting transfers between devices: none -> 5.49 us  [the longest x2 2.75 us: per_device(): on, back = (lax.ppermute(on, 'x', right), lax.ppermute(back, 'x', left))]
    pallas_call x1 -> x3, Pallas kernels: 0.18 us -> 4.53 us  [the longest x1 4.31 us: per_device(): pl.pallas_call(rest_kernel, in_specs=[hbm] * 2 + [vmem] * 3, out_shape=[s...]
    pallas_call x1, Pallas kernels: 8.97 us -> 5.49 us  [per_device(): pl.pallas_call(functools.partial(grads_kernel, groups), in_specs=[hbm] *...]
  transfers between devices with their start and end apart: 3 -> 7, of which waited for: 1 -> 2; matrix products, arithmetic and copies ran while one was open for 0% -> 0% of each run, Pallas kernels for 10% -> 14%
where the time goes in v3:
time: 99.8 us; the launch traced here: 99.4 us
  blocking collectives  58 us (58%)
  Pallas kernels  20.8 us (21%)
  starting transfers between devices  11.1 us (11%)
  waiting for transfers between devices  8.05 us (8%)
    all_to_all x1, blocking collectives, per_device(): arrived = lax.all_to_all(fields, ('x', 'zh'), 0, 0, tiled=True)  21.9 us
    all_to_all x1, blocking collectives, per_device(): line = lax.all_to_all(line, ('zh', 'y', 'zl', 'c'), 0, 0, tiled=True)  20.5 us
    all_to_all x1, blocking collectives, per_device(): grads = lax.all_to_all(grads, ('x', 'zh'), 0, 0, tiled=True)  15.6 us
    pallas_call x1, Pallas kernels, per_device(): pl.pallas_call(functools.partial(decode_kernel, groups, scale), grid=(cel...  8.89 us
    ppermute x2, waiting for transfers between devices, per_device(): on, back = (lax.ppermute(on, 'x', right), lax.ppermute(back, 'x', left))  6.83 us
    pallas_call x1, Pallas kernels, per_device(): pl.pallas_call(functools.partial(grads_kernel, groups), in_specs=[hbm] *...  5.49 us
    pallas_call x1, Pallas kernels, per_device(): pl.pallas_call(rest_kernel, in_specs=[hbm] * 2 + [vmem] * 3, out_shape=[s...  4.31 us
    ppermute x1, starting transfers between devices, per_device(): other_latent = lax.ppermute(latent, 'c', swap)  3.33 us
  transfers between devices with their start and end apart: 7, of which 2 were waited for; matrix products, arithmetic and copies ran while one was open for 0% of the time, Pallas kernels for 14%

profile of v3, /device:TPU:1, one launch (start us, length us, event | category | flops | bytes accessed | tf_op | source)
XLA Modules:
  0.0 99.4 jit_solution(1184578095631532582)
XLA Ops:
  0.6 3.3 %collective-permute-start = (bf16[1,1536,1024]{2,1,0:T(8,128)(2,1)}, bf16[1,1536,1024]{2,1,0:T(8,128)(2,1)}, u32[]{:S(2)}, u32[]{:S(2)}) collective-permute-start(bf16[1,1536,1024]{2,1,0:T(8,128)(2,1)} %own_latent_hbm.3), channel_id=1, source_target_pairs={{0,1},{1,0},{2,3},{3,2},{4,5},{5,4},{6,7},{7,6},{8,9},{9,8},{10,11... | collective-permute-start | bytes 9437192 | tf_op jit(solution)/shard_map/ppermute | solution.py:231
  4.0 0.0 copy-start
  4.0 0.0 copy-start.1
  4.0 8.9 %decode.1 = (bf16[1536,1536]{1,0:T(8,128)(2,1)}, bf16[1536,512]{1,0:T(8,128)(2,1)}, bf16[16,24,384]{2,1,0:T(8,128)(2,1)}, f32[32,384]{1,0:T(8,128)}) custom-call(bf16[1,1536,1024]{2,1,0:T(8,128)(2,1)} %own_latent_hbm.3, bf16[1024,1024]{1,0:T(8,128)(2,1)} %w_in_ref.1, bf16[96,1024]{1,0:T(8,128)(2,1)} %bitcast.1, bf16[96,1536]{1,0:T(8,128)(2,1)} %target_ref.1, ...), custom_call_target="tpu_custom_call" | custom-call | tf_op jit(solution)/shard_map/decode/pallas_call | solution.py:202
  12.9 0.1 collective-permute-start.1
  13.0 21.9 %all_to_all.15.fields_ref = bf16[16,24,384]{2,1,0:T(8,128)(2,1)S(1)} all-to-all(bf16[16,24,384]{2,1,0:T(8,128)(2,1)} %get-tuple-element.18), channel_id=1, replica_groups=mesh['x'=4,'zh'=4,'y'=4,'zl'=2,'c'=2] {'x','zh'}, dimensions={0} | all-to-all | bytes 589824 | tf_op jit(solution)/shard_map/all_to_all | solution.py:229
  34.8 0.0 copy-start.2
  34.8 0.8 copy-done.2
  35.6 1.2 %pair.1 = bf16[16,24,384]{2,1,0:T(8,128)(2,1)S(1)} custom-call(bf16[16,24,384]{2,1,0:T(8,128)(2,1)S(1)} %all_to_all.15.fields_ref, f32[32,384]{1,0:T(8,128)S(1)} %copy-done.2), custom_call_target="tpu_custom_call" | custom-call | tf_op jit(solution)/shard_map/pair/pallas_call | solution.py:233
  36.8 15.6 %all_to_all.16.own_fields_ref = bf16[16,24,384]{2,1,0:T(8,128)(2,1)S(1)} all-to-all(bf16[16,24,384]{2,1,0:T(8,128)(2,1)S(1)} %pair.1), channel_id=1, replica_groups=mesh['x'=4,'zh'=4,'y'=4,'zl'=2,'c'=2] {'x','zh'}, dimensions={0} | all-to-all | bytes 589824 | tf_op jit(solution)/shard_map/all_to_all | solution.py:241
  52.4 2.2 %collective-permute-start.2 = (bf16[16,24,384]{2,1,0:T(8,128)(2,1)S(1)}, bf16[16,24,384]{2,1,0:T(8,128)(2,1)S(1)}, u32[]{:S(2)}, u32[]{:S(2)}) collective-permute-start(bf16[16,24,384]{2,1,0:T(8,128)(2,1)S(1)} %all_to_all.16.own_fields_ref), channel_id=1, source_target_pairs={{0,1},{1,0},{2,3},{3,2},{4,5},{5,4},{6,7},{7,6},{8,9},{9,8},{10,11... | collective-permute-start | bytes 884744 | tf_op jit(solution)/shard_map/ppermute | solution.py:242
  54.6 1.2 %collective-permute-done.2.other_fields_ref = bf16[16,24,384]{2,1,0:T(8,128)(2,1)S(1)} collective-permute-done((bf16[16,24,384]{2,1,0:T(8,128)(2,1)S(1)}, bf16[16,24,384]{2,1,0:T(8,128)(2,1)S(1)}, u32[]{:S(2)}, u32[]{:S(2)}) %collective-permute-start.2) | collective-permute-done | bytes 294944 | tf_op jit(solution)/shard_map/ppermute | solution.py:242
  55.8 0.0 collective-permute-done.1.other_slope_hbm
  55.8 0.0 collective-permute-done.other_latent_hbm
  55.8 0.0 copy-done
  55.8 0.0 copy-done.1
  55.8 5.5 %grad_pre.1 = (bf16[1536,512]{1,0:T(8,128)(2,1)S(1)}, bf16[1536,512]{1,0:T(8,128)(2,1)S(1)}, f32[128,1024]{1,0:T(8,128)S(1)}, bf16[128,640]{1,0:T(8,128)(2,1)S(1)}, bf16[128,640]{1,0:T(8,128)(2,1)S(1)}) custom-call(bf16[1536,1536]{1,0:T(8,128)(2,1)} %get-tuple-element.16.kept_hbm, bf16[1536,512]{1,0:T(8,128)(2,1)S(1)} %collective-permute-done.1.other_slope_hbm, ...), custom_call_target="tpu_custom_call" | custom-call | tf_op jit(solution)/shard_map/grad_pre/pallas_call | solution.py:245
  61.3 0.1 collective-permute-start.3
  61.4 2.7 %collective-permute-start.4 = (bf16[128,640]{1,0:T(8,128)(2,1)S(1)}, bf16[128,640]{1,0:T(8,128)(2,1)S(1)}, u32[]{:S(2)}, u32[]{:S(2)}) collective-permute-start(bf16[128,640]{1,0:T(8,128)(2,1)S(1)} %get-tuple-element.27), channel_id=1, source_target_pairs={{0,192},{64,0},{128,64},{192,128},{1,193},{65,1},{129,65},{193,129... | collective-permute-start | bytes 491528 | tf_op jit(solution)/shard_map/ppermute | solution.py:269
  64.1 4.3 %weight_grads.1 = (f32[256,640]{1,0:T(8,128)S(1)}, f32[256,640]{1,0:T(8,128)S(1)}, f32[256,640]{1,0:T(8,128)S(1)}) custom-call(bf16[1,1536,1024]{2,1,0:T(8,128)(2,1)S(1)} %copy-done, bf16[1,1536,1024]{2,1,0:T(8,128)(2,1)} %collective-permute-done.other_latent_hbm, bf16[1536,512]{1,0:T(8,128)(2,1)S(1)} %get-tuple-element.20.own_pre, ...), custom_call_target="tpu_custom_call" | custom-call | flops 2415919104 | bytes 12582912 | tf_op jit(solution)/shard_map/weight_grads/pallas_call | solution.py:270
  68.4 0.0 collective-permute-done.3.top_ref
  68.4 0.0 collective-permute-done.4.bottom_ref
  68.4 0.1 pass_on.1
  68.5 0.1 collective-permute-start.5
  68.6 2.7 %collective-permute-start.6 = (bf16[256,640]{1,0:T(8,128)(2,1)S(1)}, bf16[256,640]{1,0:T(8,128)(2,1)S(1)}, u32[]{:S(2)}, u32[]{:S(2)}) collective-permute-start(bf16[256,640]{1,0:T(8,128)(2,1)S(1)} %get-tuple-element.29), channel_id=1, source_target_pairs={{0,192},{64,0},{128,64},{192,128},{1,193},{65,1},{129,65},{193,129... | collective-permute-start | bytes 983048 | tf_op jit(solution)/shard_map/ppermute | solution.py:286
  71.3 6.8 %collective-permute-done.5.on_ref = bf16[256,640]{1,0:T(8,128)(2,1)S(1)} collective-permute-done((bf16[256,640]{1,0:T(8,128)(2,1)S(1)}, bf16[256,640]{1,0:T(8,128)(2,1)S(1)}, u32[]{:S(2)}, u32[]{:S(2)}) %collective-permute-start.5) | collective-permute-done | bytes 327712 | tf_op jit(solution)/shard_map/ppermute | solution.py:286
  78.1 0.0 collective-permute-done.6.back_ref
  78.1 0.1 x_sum.1
  78.3 20.5 %all_to_all.17.in_ref = bf16[64,4,640]{2,1,0:T(4,128)(2,1)S(1)} all-to-all(bf16[64,4,640]{2,1,0:T(4,128)(2,1)S(1)} %x_sum.1), channel_id=1, replica_groups=mesh['x'=4,'zh'=4,'y'=4,'zl'=2,'c'=2] {'zh','y','zl','c'}, dimensions={0} | all-to-all | bytes 655360 | tf_op jit(solution)/shard_map/all_to_all | solution.py:290
  98.8 0.7 line_sum.1
Async XLA Ops:
  0.6 55.2 %collective-permute-start = (bf16[1,1536,1024]{2,1,0:T(8,128)(2,1)}, bf16[1,1536,1024]{2,1,0:T(8,128)(2,1)}, u32[]{:S(2)}, u32[]{:S(2)}) collective-permute-start(bf16[1,1536,1024]{2,1,0:T(8,128)(2,1)} %own_latent_hbm.3), channel_id=1, source_target_pairs={{0,1},{1,0},{2,3},{3,2},{4,5},{5,4},{6,7},{7,6},{8,9},{9,8},{10,11... | collective-permute-start | bytes 9437192 | tf_op jit(solution)/shard_map/ppermute | solution.py:231
  4.0 51.9 %copy-start = (bf16[1,1536,1024]{2,1,0:T(8,128)(2,1)S(1)}, bf16[1,1536,1024]{2,1,0:T(8,128)(2,1)}, u32[]{:S(2)}) copy-start(bf16[1,1536,1024]{2,1,0:T(8,128)(2,1)} %own_latent_hbm.3) | copy-start | bytes 9437188
  4.0 51.9 %copy-start.1 = (bf16[1024,96]{0,1:T(8,128)(2,1)S(1)}, bf16[1024,96]{0,1:T(8,128)(2,1)}, u32[]{:S(2)}) copy-start(bf16[1024,96]{0,1:T(8,128)(2,1)} %param.7) | copy-start | bytes 589828
  12.9 43.0 %collective-permute-start.1 = (bf16[1536,512]{1,0:T(8,128)(2,1)}, bf16[1536,512]{1,0:T(8,128)(2,1)S(1)}, u32[]{:S(2)}, u32[]{:S(2)}) collective-permute-start(bf16[1536,512]{1,0:T(8,128)(2,1)} %get-tuple-element.17), channel_id=1, source_target_pairs={{0,1},{1,0},{2,3},{3,2},{4,5},{5,4},{6,7},{7,6},{8,9},{9,8},{10,11... | collective-permute-start | bytes 4718600 | tf_op jit(solution)/shard_map/ppermute | solution.py:230
  34.8 0.8 copy-start.2
  52.4 3.4 %collective-permute-start.2 = (bf16[16,24,384]{2,1,0:T(8,128)(2,1)S(1)}, bf16[16,24,384]{2,1,0:T(8,128)(2,1)S(1)}, u32[]{:S(2)}, u32[]{:S(2)}) collective-permute-start(bf16[16,24,384]{2,1,0:T(8,128)(2,1)S(1)} %all_to_all.16.own_fields_ref), channel_id=1, source_target_pairs={{0,1},{1,0},{2,3},{3,2},{4,5},{5,4},{6,7},{7,6},{8,9},{9,8},{10,11... | collective-permute-start | bytes 884744 | tf_op jit(solution)/shard_map/ppermute | solution.py:242
  61.3 7.1 %collective-permute-start.3 = (bf16[128,640]{1,0:T(8,128)(2,1)S(1)}, bf16[128,640]{1,0:T(8,128)(2,1)S(1)}, u32[]{:S(2)}, u32[]{:S(2)}) collective-permute-start(bf16[128,640]{1,0:T(8,128)(2,1)S(1)} %get-tuple-element.26), channel_id=1, source_target_pairs={{0,64},{64,128},{128,192},{192,0},{1,65},{65,129},{129,193},{193,1... | collective-permute-start | bytes 491528 | tf_op jit(solution)/shard_map/ppermute | solution.py:269
  61.4 7.0 %collective-permute-start.4 = (bf16[128,640]{1,0:T(8,128)(2,1)S(1)}, bf16[128,640]{1,0:T(8,128)(2,1)S(1)}, u32[]{:S(2)}, u32[]{:S(2)}) collective-permute-start(bf16[128,640]{1,0:T(8,128)(2,1)S(1)} %get-tuple-element.27), channel_id=1, source_target_pairs={{0,192},{64,0},{128,64},{192,128},{1,193},{65,1},{129,65},{193,129... | collective-permute-start | bytes 491528 | tf_op jit(solution)/shard_map/ppermute | solution.py:269
  68.5 9.6 %collective-permute-start.5 = (bf16[256,640]{1,0:T(8,128)(2,1)S(1)}, bf16[256,640]{1,0:T(8,128)(2,1)S(1)}, u32[]{:S(2)}, u32[]{:S(2)}) collective-permute-start(bf16[256,640]{1,0:T(8,128)(2,1)S(1)} %get-tuple-element.28), channel_id=1, source_target_pairs={{0,64},{64,128},{128,192},{192,0},{1,65},{65,129},{129,193},{193,1... | collective-permute-start | bytes 983048 | tf_op jit(solution)/shard_map/ppermute | solution.py:286
  68.6 9.5 %collective-permute-start.6 = (bf16[256,640]{1,0:T(8,128)(2,1)S(1)}, bf16[256,640]{1,0:T(8,128)(2,1)S(1)}, u32[]{:S(2)}, u32[]{:S(2)}) collective-permute-start(bf16[256,640]{1,0:T(8,128)(2,1)S(1)} %get-tuple-element.29), channel_id=1, source_target_pairs={{0,192},{64,0},{128,64},{192,128},{1,193},{65,1},{129,65},{193,129... | collective-permute-start | bytes 983048 | tf_op jit(solution)/shard_map/ppermute | solution.py:286

commit v4 on v3

--- a/solution.py
+++ b/solution.py
@@ -21,21 +21,9 @@
 
 
 def decode_kernel(
-    groups, scale, latent_ref, w_in_ref, w_out_ref, target_ref, mask_ref,
-    kept_ref, other_ref, fields_ref, picked_ref, target_rows,
+    groups, latent_ref, w_in_ref, w_out_ref, kept_ref, other_ref, fields_ref,
 ):
     _, rows, lanes = fields_ref.shape
-    members = groups * groups
-
-    @pl.when(pl.program_id(0) == 0)
-    def _():
-        column = pl.multiple_of(lax.axis_index("x") * lanes, 128)
-        row = pl.multiple_of(lax.axis_index("zh") * rows, 8)
-        target_rows[...] = target_ref[:, pl.ds(column, lanes)].astype(F32)
-        picked_ref[:rows] = target_rows[pl.ds(row, rows), :]
-        weight = mask_ref[pl.ds(column, lanes)].reshape(1, lanes).astype(F32) * scale / members
-        picked_ref[rows:] = jnp.broadcast_to(weight, (8, lanes))
-
     pre = jnp.dot(latent_ref[0], w_in_ref[...], preferred_element_type=F32)
     gate = 1.0 / (1.0 + jnp.exp(-pre))
     value = pre * gate
@@ -52,9 +40,13 @@
             fields_ref[b * groups + g] = fields[g * rows : (g + 1) * rows, b * lanes : (b + 1) * lanes].astype(BF)
 
 
-def pair_kernel(fields_ref, picked_ref, out_ref, value, total):
+def pair_kernel(scale, fields_ref, target_ref, mask_ref, out_ref, target_rows, value, total):
     members, rows, lanes = fields_ref.shape
-    target, weight = picked_ref[:rows], picked_ref[rows : rows + 1]
+    column = pl.multiple_of(lax.axis_index("x") * lanes, 128)
+    row = pl.multiple_of(lax.axis_index("zh") * rows, 8)
+    target_rows[...] = target_ref[:, pl.ds(column, lanes)].astype(F32)
+    target = target_rows[pl.ds(row, rows), :]
+    weight = mask_ref[pl.ds(column, lanes)].reshape(1, lanes).astype(F32) * scale / members
     for m in range(members):
         value[m] = fields_ref[m].astype(F32)
     for r in range(0, rows, 8):
@@ -102,40 +94,42 @@
         return jnp.concatenate([total, out_term[:, self.at].T], axis=1)
 
 
-def grads_kernel(
-    groups, kept_hbm, other_slope_hbm, own_latent_hbm, other_latent_hbm, own_fields_ref, other_fields_ref,
-    w_out_ref, own_pre, other_pre, out_term, top_ref, bottom_ref, kept, other_slope, own_latent, other_latent,
-    sems, latent_sems,
-):
-    lanes, half = own_fields_ref.shape[2], other_slope.shape[1]
+def own_kernel(groups, kept_hbm, fields_ref, w_out_ref, own_pre, out_term, kept, sems):
+    lanes, half = fields_ref.shape[2], own_pre.shape[1]
     cuts = [slice(b * lanes, (b + 1) * lanes) for b in range(groups)]
-
-    def copies_of(which, source, into):
-        return [pltpu.make_async_copy(source.at[cut], into.at[cut], sems.at[which, b]) for b, cut in enumerate(cuts)]
-
-    kepts = copies_of(0, kept_hbm, kept)
-    other_slopes = copies_of(1, other_slope_hbm, other_slope)
-    latents = Rows(2, own_latent_hbm, other_latent_hbm, own_latent, other_latent, latent_sems)
-    for copy in kepts + other_slopes:
+    copies = [pltpu.make_async_copy(kept_hbm.at[cut], kept.at[cut], sems.at[b]) for b, cut in enumerate(cuts)]
+    for copy in copies:
         copy.start()
-    latents.start()
-
     at = pl.multiple_of(lax.axis_index("c") * half, 128)
     w_out = w_out_ref[:, pl.ds(at, half)]
     fields_n = w_out.shape[0]
     out_term[...] = jnp.zeros_like(out_term)
     for b, cut in enumerate(cuts):
-        grad = gathered(own_fields_ref, b, groups)
+        grad = gathered(fields_ref, b, groups)
         back = mxu(grad, w_out, 0, 0)
-        kepts[b].wait()
+        copies[b].wait()
         hidden, slope = kept[cut, : kept.shape[1] - half], kept[cut, kept.shape[1] - half :]
         own_pre[cut] = (back * slope.astype(F32)).astype(BF)
         out_term[:fields_n] += jnp.dot(grad, hidden, preferred_element_type=F32)
+
+
+def other_kernel(
+    groups, slope_hbm, own_latent_hbm, other_latent_hbm, fields_ref, w_out_ref, own_pre, out_term, other_pre, top_ref,
+    bottom_ref, slope, own_latent, other_latent, sems, latent_sems,
+):
+    lanes, half = fields_ref.shape[2], own_pre.shape[1]
+    cuts = [slice(b * lanes, (b + 1) * lanes) for b in range(groups)]
+    copies = [pltpu.make_async_copy(slope_hbm.at[cut], slope.at[cut], sems.at[b]) for b, cut in enumerate(cuts)]
+    latents = Rows(2, own_latent_hbm, other_latent_hbm, own_latent, other_latent, latent_sems)
+    for copy in copies:
+        copy.start()
+    latents.start()
+    at = pl.multiple_of(lax.axis_index("c") * half, 128)
+    w_out = w_out_ref[:, pl.ds(at, half)]
     for b, cut in enumerate(cuts):
-        back = mxu(gathered(other_fields_ref, b, groups), w_out, 0, 0)
-        other_slopes[b].wait()
-        other_pre[cut] = (back * other_slope[cut].astype(F32)).astype(BF)
-
+        back = mxu(gathered(fields_ref, b, groups), w_out, 0, 0)
+        copies[b].wait()
+        other_pre[cut] = (back * slope[cut].astype(F32)).astype(BF)
     total = latents.value(own_pre, other_pre, out_term)
     middle = top_ref.shape[0]
     top_ref[...] = total[:middle].astype(BF)
@@ -167,15 +161,22 @@
         out_ref[p] = total[rows * p : rows * (p + 1)].astype(BF)
 
 
-def last_kernel(in_ref, grad_in_ref, grad_out_ref):
-    first, second = in_ref[0].astype(F32), in_ref[1].astype(F32)
-    for z in range(2, in_ref.shape[0], 2):
-        first += in_ref[z].astype(F32)
-        second += in_ref[z + 1].astype(F32)
+def split_kernel(in_ref, keep_ref, send_ref):
+    total = in_ref[0].astype(F32)
+    for p in range(1, in_ref.shape[0]):
+        total += in_ref[p].astype(F32)
+    first = lax.axis_index("c") == 0
+    keep_ref[...] = jnp.where(first, total[:4], total[4:])
+    send_ref[...] = jnp.where(first, total[4:], total[:4])
+
+
+def join_kernel(keep_ref, came_ref, grad_in_ref, grad_out_ref):
+    keep, came = keep_ref[...], came_ref[...]
     half = grad_in_ref.shape[1] // 2
-    grad_in_ref[:, :half] = first[:, :half]
-    grad_in_ref[:, half:] = second[:, :half]
-    grad_out_ref[...] = (first + second)[:, half : half + grad_out_ref.shape[1]]
+    first = lax.axis_index("c") == 0
+    grad_in_ref[:, :half] = jnp.where(first, keep[:, :half], came[:, :half])
+    grad_in_ref[:, half:] = jnp.where(first, came[:, :half], keep[:, :half])
+    grad_out_ref[...] = (keep + came)[:, half : half + grad_out_ref.shape[1]]
 
 
 def shape(*dims, dtype=BF):
@@ -199,70 +200,72 @@
     step = 2 * block
     halves = pl.BlockSpec((step, half), lambda i: (i, 0))
 
-    kept, other_slope, fields, picked = pl.pallas_call(
-        functools.partial(decode_kernel, groups, scale),
+    kept, other_slope, fields = pl.pallas_call(
+        functools.partial(decode_kernel, groups),
         grid=(cells // step,),
         in_specs=[
             pl.BlockSpec((1, step, depth), lambda i: (0, i, 0)),
             whole(depth, hidden_size),
             whole(fields_n, hidden_size),
-            whole(fields_n, cells),
-            whole(cells),
         ],
         out_specs=[
             pl.BlockSpec((step, hidden_size + half), lambda i: (i, 0)),
             halves,
             pl.BlockSpec((2 * groups, rows, block), lambda i: (i, 0, 0)),
-            whole(rows + 8, block),
         ],
         out_shape=[
             shape(cells, hidden_size + half),
             shape(cells, half),
             shape(members, rows, block),
-            shape(rows + 8, block, dtype=F32),
-        ],
-        scratch_shapes=[pltpu.VMEM((fields_n, block), F32)],
+        ],
         compiler_params=params(58),
         name="decode",
-    )(latent, w_in, w_out_t, target, cell_mask)
-
+    )(latent, w_in, w_out_t)
+
+    latent, fields = lax.optimization_barrier((latent, fields))
     arrived = lax.all_to_all(fields, ("x", "zh"), 0, 0, tiled=True)
     other_slope = lax.ppermute(other_slope, "c", swap)
     other_latent = lax.ppermute(latent, "c", swap)
 
     grads = pl.pallas_call(
-        pair_kernel,
+        functools.partial(pair_kernel, scale),
         out_shape=shape(members, rows, block),
-        scratch_shapes=[pltpu.VMEM((members, rows, block), F32), pltpu.VMEM((members, rows, block), F32)],
+        scratch_shapes=[
+            pltpu.VMEM((fields_n, block), F32),
+            pltpu.VMEM((members, rows, block), F32),
+            pltpu.VMEM((members, rows, block), F32),
+        ],
         compiler_params=params(16),
         name="pair",
-    )(arrived, picked)
+    )(arrived, target, cell_mask)
 
     grads = lax.all_to_all(grads, ("x", "zh"), 0, 0, tiled=True)
     other_grads = lax.ppermute(grads, "c", swap)
 
     quarter = depth // 4
-    own_pre, other_pre, out_term, top, bottom = pl.pallas_call(
-        functools.partial(grads_kernel, groups),
-        in_specs=[hbm] * 4 + [vmem] * 3,
-        out_shape=[
-            shape(cells, half),
-            shape(cells, half),
-            shape(128, hidden_size, dtype=F32),
-            shape(quarter // 2, wide),
-            shape(quarter // 2, wide),
-        ],
+    own_pre, out_term = pl.pallas_call(
+        functools.partial(own_kernel, groups),
+        in_specs=[hbm] + [vmem] * 2,
+        out_shape=[shape(cells, half), shape(128, hidden_size, dtype=F32)],
+        scratch_shapes=[pltpu.VMEM((cells, hidden_size + half), BF), pltpu.SemaphoreType.DMA((groups,))],
+        compiler_params=params(50),
+        cost_estimate=pl.CostEstimate(flops=4 * cells * half * fields_n, bytes_accessed=6 << 20, transcendentals=0),
+        name="own_grad_pre",
+    )(kept, grads, w_out_t)
+    other_pre, top, bottom = pl.pallas_call(
+        functools.partial(other_kernel, groups),
+        in_specs=[hbm] * 3 + [vmem] * 4,
+        out_shape=[shape(cells, half), shape(quarter // 2, wide), shape(quarter // 2, wide)],
         scratch_shapes=[
-            pltpu.VMEM((cells, hidden_size + half), BF),
             pltpu.VMEM((cells, half), BF),
             pltpu.VMEM((cells, quarter), BF),
             pltpu.VMEM((cells, quarter), BF),
-            pltpu.SemaphoreType.DMA((2, groups)),
+            pltpu.SemaphoreType.DMA((groups,)),
             pltpu.SemaphoreType.DMA((2,)),
         ],
         compiler_params=params(40),
-        name="grad_pre",
-    )(kept, other_slope, latent, other_latent, grads, other_grads, w_out_t)
+        name="other_grad_pre",
+    )(other_slope, latent, other_latent, other_grads, w_out_t, own_pre, out_term)
 
     right = [(i, (i + 1) % 4) for i in range(4)]
     left = [(i, (i + 3) % 4) for i in range(4)]
@@ -285,15 +288,18 @@
     )(on, back, top, bottom)
     on, back = lax.ppermute(on, "x", right), lax.ppermute(back, "x", left)
     line = pl.pallas_call(
-        x_kernel, out_shape=shape(64, 4, wide), compiler_params=params(16), name="x_sum"
+        x_kernel, out_shape=shape(32, 8, wide), compiler_params=params(16), name="x_sum"
     )(stay, on, back)
-    line = lax.all_to_all(line, ("zh", "y", "zl", "c"), 0, 0, tiled=True)
+    line = lax.all_to_all(line, ("zh", "y", "zl"), 0, 0, tiled=True)
+    few = shape(4, wide, dtype=F32)
+    keep, send = pl.pallas_call(split_kernel, out_shape=[few, few], compiler_params=params(16), name="yz_sum")(line)
+    came = lax.ppermute(send, "c", swap)
     return pl.pallas_call(
-        last_kernel,
+        join_kernel,
         out_shape=[shape(4, hidden_size, dtype=F32), shape(4, fields_n, dtype=F32)],
         compiler_params=params(16),
-        name="line_sum",
-    )(line)
+        name="join",
+    )(keep, came)
 
 
 def solution(mesh):

time: 99.8 us -> 99 us (level)
  blocking collectives: 58 us -> 52.2 us
  starting transfers between devices: 11.1 us -> 16.2 us
    all_to_all x1, blocking collectives: 20.5 us -> 15.2 us  [per_device(): line = lax.all_to_all(line, ('zh', 'y', 'zl'), 0, 0, tiled=True)]
    ppermute x0 -> x1, starting transfers between devices: none -> 4.21 us  [per_device(): came = lax.ppermute(send, 'c', swap)]
    ppermute x1, waiting for transfers between devices: 1.21 us -> 0.01 us  [per_device(): other_grads = lax.ppermute(grads, 'c', swap)]
    pallas_call x5 -> x7, Pallas kernels: 16.4 us -> 17.3 us  [the longest x1 8.66 us: per_device(): pl.pallas_call(functools.partial(decode_kernel, groups), grid=(cells // s...]
  transfers between devices with their start and end apart: 7 -> 8, of which waited for: 2 -> 3; matrix products, arithmetic and copies ran while one was open for 0% -> 0% of each run, Pallas kernels for 14% -> 8%
where the time goes in v4:
time: 99 us; the launch traced here: 98.7 us
  blocking collectives  52.2 us (53%)
  Pallas kernels  21.1 us (21%)
  starting transfers between devices  16.2 us (16%)
  waiting for transfers between devices  8.48 us (9%)
    all_to_all x1, blocking collectives, per_device(): arrived = lax.all_to_all(fields, ('x', 'zh'), 0, 0, tiled=True)  21.9 us
    all_to_all x1, blocking collectives, per_device(): line = lax.all_to_all(line, ('zh', 'y', 'zl'), 0, 0, tiled=True)  15.2 us
    all_to_all x1, blocking collectives, per_device(): grads = lax.all_to_all(grads, ('x', 'zh'), 0, 0, tiled=True)  15.2 us
    pallas_call x1, Pallas kernels, per_device(): pl.pallas_call(functools.partial(decode_kernel, groups), grid=(cells // s...  8.66 us
    ppermute x2, waiting for transfers between devices, per_device(): on, back = (lax.ppermute(on, 'x', right), lax.ppermute(back, 'x', left))  6.99 us
    ppermute x1, starting transfers between devices, per_device(): came = lax.ppermute(send, 'c', swap)  4.21 us
    pallas_call x1, Pallas kernels, per_device(): pl.pallas_call(rest_kernel, in_specs=[hbm] * 2 + [vmem] * 3, out_shape=[s...  3.7 us
    pallas_call x1, Pallas kernels, per_device(): pl.pallas_call(functools.partial(other_kernel, groups), in_specs=[hbm] *...  3.48 us
  transfers between devices with their start and end apart: 8, of which 3 were waited for; matrix products, arithmetic and copies ran while one was open for 0% of the time, Pallas kernels for 8%

profile of v4, /device:TPU:1, one launch (start us, length us, event | category | flops | bytes accessed | tf_op | source)
XLA Modules:
  0.0 98.7 jit_solution(3979775865946195701)
XLA Ops:
  0.6 0.0 copy-start
  0.6 0.0 copy-start.2
  0.7 0.0 copy-start.3
  0.7 8.7 %decode.1 = (bf16[1536,1536]{1,0:T(8,128)(2,1)}, bf16[1536,512]{1,0:T(8,128)(2,1)}, bf16[16,24,384]{2,1,0:T(8,128)(2,1)}) custom-call(bf16[1,1536,1024]{2,1,0:T(8,128)(2,1)} %own_latent_hbm.1, bf16[1024,1024]{1,0:T(8,128)(2,1)} %w_in_ref.1, bf16[96,1024]{1,0:T(8,128)(2,1)} %bitcast.1), custom_call_target="tpu_custom_call" | custom-call | tf_op jit(solution)/shard_map/decode/pallas_call | solution.py:203
  9.3 0.0 copy-start.1
  9.3 0.0 copy-done
  9.3 3.3 %collective-permute-start = (bf16[1,1536,1024]{2,1,0:T(8,128)(2,1)S(1)}, bf16[1,1536,1024]{2,1,0:T(8,128)(2,1)S(1)}, u32[]{:S(2)}, u32[]{:S(2)}) collective-permute-start(bf16[1,1536,1024]{2,1,0:T(8,128)(2,1)S(1)} %copy-done), channel_id=1, source_target_pairs={{0,1},{1,0},{2,3},{3,2},{4,5},{5,4},{6,7},{7,6},{8,9},{9,8},{10,11... | collective-permute-start | bytes 9437192 | tf_op jit(solution)/shard_map/ppermute | solution.py:228
  12.6 0.1 collective-permute-start.1
  12.7 21.9 %all_to_all.15.fields_ref = bf16[16,24,384]{2,1,0:T(8,128)(2,1)S(1)} all-to-all(bf16[16,24,384]{2,1,0:T(8,128)(2,1)} %get-tuple-element.22), channel_id=1, replica_groups=mesh['x'=4,'zh'=4,'y'=4,'zl'=2,'c'=2] {'x','zh'}, dimensions={0} | all-to-all | bytes 589824 | tf_op jit(solution)/shard_map/all_to_all | solution.py:226
  34.6 0.0 copy-done.2
  34.6 0.0 copy-done.3
  34.6 1.2 %pair.1 = bf16[16,24,384]{2,1,0:T(8,128)(2,1)S(1)} custom-call(bf16[16,24,384]{2,1,0:T(8,128)(2,1)S(1)} %all_to_all.15.fields_ref, bf16[96,1536]{1,0:T(8,128)(2,1)S(1)} %copy-done.2, s32[1536]{0:T(1024)S(1)} %copy-done.3), custom_call_target="tpu_custom_call" | custom-call | tf_op jit(solution)/shard_map/pair/pallas_call | solution.py:230
  35.8 15.2 %all_to_all.16.fields_ref = bf16[16,24,384]{2,1,0:T(8,128)(2,1)S(1)} all-to-all(bf16[16,24,384]{2,1,0:T(8,128)(2,1)S(1)} %pair.1), channel_id=1, replica_groups=mesh['x'=4,'zh'=4,'y'=4,'zl'=2,'c'=2] {'x','zh'}, dimensions={0} | all-to-all | bytes 589824 | tf_op jit(solution)/shard_map/all_to_all | solution.py:242
  51.0 3.0 %collective-permute-start.2 = (bf16[16,24,384]{2,1,0:T(8,128)(2,1)S(1)}, bf16[16,24,384]{2,1,0:T(8,128)(2,1)S(1)}, u32[]{:S(2)}, u32[]{:S(2)}) collective-permute-start(bf16[16,24,384]{2,1,0:T(8,128)(2,1)S(1)} %all_to_all.16.fields_ref), channel_id=1, source_target_pairs={{0,1},{1,0},{2,3},{3,2},{4,5},{5,4},{6,7},{7,6},{8,9},{9,8},{10,11... | collective-permute-start | bytes 884744 | tf_op jit(solution)/shard_map/ppermute | solution.py:243
  54.0 0.0 copy-done.1
  54.0 3.2 %own_grad_pre.1 = (bf16[1536,512]{1,0:T(8,128)(2,1)S(1)}, f32[128,1024]{1,0:T(8,128)S(1)}) custom-call(bf16[1536,1536]{1,0:T(8,128)(2,1)} %get-tuple-element.21.kept_hbm, bf16[16,24,384]{2,1,0:T(8,128)(2,1)S(1)} %all_to_all.16.fields_ref, bf16[96,1024]{1,0:T(8,128)(2,1)S(1)} %bitcast.2), custom_call_target="tpu_custom_call" | custom-call | flops 301989888 | bytes 6291456 | tf_op jit(solution)/shard_map/own_grad_pre/pallas_call | solution.py:246
  57.2 0.0 collective-permute-done.2.fields_ref
  57.2 0.0 collective-permute-done.1.slope_hbm
  57.2 0.0 collective-permute-done.other_latent_hbm
  57.2 3.5 %other_grad_pre.1 = (bf16[1536,512]{1,0:T(8,128)(2,1)S(1)}, bf16[128,640]{1,0:T(8,128)(2,1)S(1)}, bf16[128,640]{1,0:T(8,128)(2,1)S(1)}) custom-call(bf16[1536,512]{1,0:T(8,128)(2,1)S(1)} %collective-permute-done.1.slope_hbm, bf16[1,1536,1024]{2,1,0:T(8,128)(2,1)S(1)} %copy-done, bf16[1,1536,1024]{2,1,0:T(8,128)(2,1)S(1)} %collective-permute-done.other_latent_hbm, ...), custom_call_target="tpu_custom_call" | custom-call | tf_op jit(solution)/shard_map/other_grad_pre/pallas_call | solution.py:255
  60.7 0.1 collective-permute-start.3
  60.8 2.7 %collective-permute-start.4 = (bf16[128,640]{1,0:T(8,128)(2,1)S(1)}, bf16[128,640]{1,0:T(8,128)(2,1)S(1)}, u32[]{:S(2)}, u32[]{:S(2)}) collective-permute-start(bf16[128,640]{1,0:T(8,128)(2,1)S(1)} %get-tuple-element.31), channel_id=1, source_target_pairs={{0,192},{64,0},{128,64},{192,128},{1,193},{65,1},{129,65},{193,129... | collective-permute-start | bytes 491528 | tf_op jit(solution)/shard_map/ppermute | solution.py:272
  63.5 3.7 %weight_grads.1 = (f32[256,640]{1,0:T(8,128)S(1)}, f32[256,640]{1,0:T(8,128)S(1)}, f32[256,640]{1,0:T(8,128)S(1)}) custom-call(bf16[1,1536,1024]{2,1,0:T(8,128)(2,1)S(1)} %copy-done, bf16[1,1536,1024]{2,1,0:T(8,128)(2,1)S(1)} %collective-permute-done.other_latent_hbm, bf16[1536,512]{1,0:T(8,128)(2,1)S(1)} %get-tuple-element.23.own_pre, ...), custom_call_target="tpu_custom_call" | custom-call | flops 2415919104 | bytes 12582912 | tf_op jit(solution)/shard_map/weight_grads/pallas_call | solution.py:273
  67.2 0.7 collective-permute-done.3.top_ref
  67.8 0.0 collective-permute-done.4.bottom_ref
  67.8 0.1 pass_on.1
  67.9 0.1 collective-permute-start.5
  68.0 2.7 %collective-permute-start.6 = (bf16[256,640]{1,0:T(8,128)(2,1)S(1)}, bf16[256,640]{1,0:T(8,128)(2,1)S(1)}, u32[]{:S(2)}, u32[]{:S(2)}) collective-permute-start(bf16[256,640]{1,0:T(8,128)(2,1)S(1)} %get-tuple-element.33), channel_id=1, source_target_pairs={{0,192},{64,0},{128,64},{192,128},{1,193},{65,1},{129,65},{193,129... | collective-permute-start | bytes 983048 | tf_op jit(solution)/shard_map/ppermute | solution.py:289
  70.7 7.0 %collective-permute-done.5.on_ref = bf16[256,640]{1,0:T(8,128)(2,1)S(1)} collective-permute-done((bf16[256,640]{1,0:T(8,128)(2,1)S(1)}, bf16[256,640]{1,0:T(8,128)(2,1)S(1)}, u32[]{:S(2)}, u32[]{:S(2)}) %collective-permute-start.5) | collective-permute-done | bytes 327712 | tf_op jit(solution)/shard_map/ppermute | solution.py:289
  77.7 0.0 collective-permute-done.6.back_ref
  77.7 0.1 x_sum.1
  77.8 15.2 %all_to_all.17.in_ref = bf16[32,8,640]{2,1,0:T(8,128)(2,1)S(1)} all-to-all(bf16[32,8,640]{2,1,0:T(8,128)(2,1)S(1)} %x_sum.1), channel_id=1, replica_groups=mesh['x'=4,'zh'=4,'y'=4,'zl'=2,'c'=2] {'zh','y','zl'}, dimensions={0} | all-to-all | bytes 655360 | tf_op jit(solution)/shard_map/all_to_all | solution.py:293
  93.0 0.1 yz_sum.1
  93.1 4.2 %collective-permute-start.7 = (f32[4,640]{1,0:T(4,128)S(1)}, f32[4,640]{1,0:T(4,128)S(1)}, u32[]{:S(2)}, u32[]{:S(2)}) collective-permute-start(f32[4,640]{1,0:T(4,128)S(1)} %get-tuple-element.35), channel_id=1, source_target_pairs={{0,1},{1,0},{2,3},{3,2},{4,5},{5,4},{6,7},{7,6},{8,9},{9,8},{10,11... | collective-permute-start | bytes 30728 | tf_op jit(solution)/shard_map/ppermute | solution.py:296
  97.3 0.8 collective-permute-done.7.came_ref
  98.1 0.6 join.1
Async XLA Ops:
  0.6 8.7 %copy-start = (bf16[1,1536,1024]{2,1,0:T(8,128)(2,1)S(1)}, bf16[1,1536,1024]{2,1,0:T(8,128)(2,1)}, u32[]{:S(2)}) copy-start(bf16[1,1536,1024]{2,1,0:T(8,128)(2,1)} %own_latent_hbm.1) | copy-start | bytes 9437188
  0.6 34.0 %copy-start.2 = (bf16[96,1536]{1,0:T(8,128)(2,1)S(1)}, bf16[96,1536]{1,0:T(8,128)(2,1)}, u32[]{:S(2)}) copy-start(bf16[96,1536]{1,0:T(8,128)(2,1)} %target_ref.1) | copy-start | bytes 884740
  0.7 34.0 %copy-start.3 = (s32[1536]{0:T(1024)S(1)}, s32[1536]{0:T(1024)}, u32[]{:S(2)}) copy-start(s32[1536]{0:T(1024)} %mask_ref.1) | copy-start | bytes 18436
  9.3 44.7 %copy-start.1 = (bf16[1024,96]{0,1:T(8,128)(2,1)S(1)}, bf16[1024,96]{0,1:T(8,128)(2,1)}, u32[]{:S(2)}) copy-start(bf16[1024,96]{0,1:T(8,128)(2,1)} %param.7) | copy-start | bytes 589828
  9.3 47.9 %collective-permute-start = (bf16[1,1536,1024]{2,1,0:T(8,128)(2,1)S(1)}, bf16[1,1536,1024]{2,1,0:T(8,128)(2,1)S(1)}, u32[]{:S(2)}, u32[]{:S(2)}) collective-permute-start(bf16[1,1536,1024]{2,1,0:T(8,128)(2,1)S(1)} %copy-done), channel_id=1, source_target_pairs={{0,1},{1,0},{2,3},{3,2},{4,5},{5,4},{6,7},{7,6},{8,9},{9,8},{10,11... | collective-permute-start | bytes 9437192 | tf_op jit(solution)/shard_map/ppermute | solution.py:228
  12.6 44.5 %collective-permute-start.1 = (bf16[1536,512]{1,0:T(8,128)(2,1)}, bf16[1536,512]{1,0:T(8,128)(2,1)S(1)}, u32[]{:S(2)}, u32[]{:S(2)}) collective-permute-start(bf16[1536,512]{1,0:T(8,128)(2,1)} %get-tuple-element.24), channel_id=1, source_target_pairs={{0,1},{1,0},{2,3},{3,2},{4,5},{5,4},{6,7},{7,6},{8,9},{9,8},{10,11... | collective-permute-start | bytes 4718600 | tf_op jit(solution)/shard_map/ppermute | solution.py:227
  51.0 6.2 %collective-permute-start.2 = (bf16[16,24,384]{2,1,0:T(8,128)(2,1)S(1)}, bf16[16,24,384]{2,1,0:T(8,128)(2,1)S(1)}, u32[]{:S(2)}, u32[]{:S(2)}) collective-permute-start(bf16[16,24,384]{2,1,0:T(8,128)(2,1)S(1)} %all_to_all.16.fields_ref), channel_id=1, source_target_pairs={{0,1},{1,0},{2,3},{3,2},{4,5},{5,4},{6,7},{7,6},{8,9},{9,8},{10,11... | collective-permute-start | bytes 884744 | tf_op jit(solution)/shard_map/ppermute | solution.py:243
  60.7 7.1 %collective-permute-start.3 = (bf16[128,640]{1,0:T(8,128)(2,1)S(1)}, bf16[128,640]{1,0:T(8,128)(2,1)S(1)}, u32[]{:S(2)}, u32[]{:S(2)}) collective-permute-start(bf16[128,640]{1,0:T(8,128)(2,1)S(1)} %get-tuple-element.30), channel_id=1, source_target_pairs={{0,64},{64,128},{128,192},{192,0},{1,65},{65,129},{129,193},{193,1... | collective-permute-start | bytes 491528 | tf_op jit(solution)/shard_map/ppermute | solution.py:272
  60.8 7.0 %collective-permute-start.4 = (bf16[128,640]{1,0:T(8,128)(2,1)S(1)}, bf16[128,640]{1,0:T(8,128)(2,1)S(1)}, u32[]{:S(2)}, u32[]{:S(2)}) collective-permute-start(bf16[128,640]{1,0:T(8,128)(2,1)S(1)} %get-tuple-element.31), channel_id=1, source_target_pairs={{0,192},{64,0},{128,64},{192,128},{1,193},{65,1},{129,65},{193,129... | collective-permute-start | bytes 491528 | tf_op jit(solution)/shard_map/ppermute | solution.py:272
  67.9 9.7 %collective-permute-start.5 = (bf16[256,640]{1,0:T(8,128)(2,1)S(1)}, bf16[256,640]{1,0:T(8,128)(2,1)S(1)}, u32[]{:S(2)}, u32[]{:S(2)}) collective-permute-start(bf16[256,640]{1,0:T(8,128)(2,1)S(1)} %get-tuple-element.32), channel_id=1, source_target_pairs={{0,64},{64,128},{128,192},{192,0},{1,65},{65,129},{129,193},{193,1... | collective-permute-start | bytes 983048 | tf_op jit(solution)/shard_map/ppermute | solution.py:289
  68.0 9.7 %collective-permute-start.6 = (bf16[256,640]{1,0:T(8,128)(2,1)S(1)}, bf16[256,640]{1,0:T(8,128)(2,1)S(1)}, u32[]{:S(2)}, u32[]{:S(2)}) collective-permute-start(bf16[256,640]{1,0:T(8,128)(2,1)S(1)} %get-tuple-element.33), channel_id=1, source_target_pairs={{0,192},{64,0},{128,64},{192,128},{1,193},{65,1},{129,65},{193,129... | collective-permute-start | bytes 983048 | tf_op jit(solution)/shard_map/ppermute | solution.py:289
  93.1 5.0 %collective-permute-start.7 = (f32[4,640]{1,0:T(4,128)S(1)}, f32[4,640]{1,0:T(4,128)S(1)}, u32[]{:S(2)}, u32[]{:S(2)}) collective-permute-start(f32[4,640]{1,0:T(4,128)S(1)} %get-tuple-element.35), channel_id=1, source_target_pairs={{0,1},{1,0},{2,3},{3,2},{4,5},{5,4},{6,7},{7,6},{8,9},{9,8},{10,11... | collective-permute-start | bytes 30728 | tf_op jit(solution)/shard_map/ppermute | solution.py:296

commit v5 on v4

--- a/solution.py
+++ b/solution.py
@@ -222,7 +222,6 @@
         name="decode",
     )(latent, w_in, w_out_t)
 
-    latent, fields = lax.optimization_barrier((latent, fields))
     arrived = lax.all_to_all(fields, ("x", "zh"), 0, 0, tiled=True)
     other_slope = lax.ppermute(other_slope, "c", swap)
     other_latent = lax.ppermute(latent, "c", swap)

time: 99 us -> 98.9 us (level)
  transfers between devices with their start and end apart: 8 -> 8, of which waited for: 3 -> 3; matrix products, arithmetic and copies ran while one was open for 0% -> 0% of each run, Pallas kernels for 8% -> 17%
where the time goes in v5:
time: 98.9 us; the launch traced here: 98.6 us
  blocking collectives  52.8 us (53%)
  Pallas kernels  21.1 us (21%)
  starting transfers between devices  15.4 us (16%)
  waiting for transfers between devices  8.47 us (9%)
    all_to_all x1, blocking collectives, per_device(): arrived = lax.all_to_all(fields, ('x', 'zh'), 0, 0, tiled=True)  21.9 us
    all_to_all x1, blocking collectives, per_device(): grads = lax.all_to_all(grads, ('x', 'zh'), 0, 0, tiled=True)  15.6 us
    all_to_all x1, blocking collectives, per_device(): line = lax.all_to_all(line, ('zh', 'y', 'zl'), 0, 0, tiled=True)  15.3 us
    pallas_call x1, Pallas kernels, per_device(): pl.pallas_call(functools.partial(decode_kernel, groups), grid=(cells // s...  8.54 us
    ppermute x2, waiting for transfers between devices, per_device(): on, back = (lax.ppermute(on, 'x', right), lax.ppermute(back, 'x', left))  6.98 us
    ppermute x1, starting transfers between devices, per_device(): came = lax.ppermute(send, 'c', swap)  4.21 us
    pallas_call x1, Pallas kernels, per_device(): pl.pallas_call(rest_kernel, in_specs=[hbm] * 2 + [vmem] * 3, out_shape=[s...  3.7 us
    pallas_call x1, Pallas kernels, per_device(): pl.pallas_call(functools.partial(other_kernel, groups), in_specs=[hbm] *...  3.48 us
  transfers between devices with their start and end apart: 8, of which 3 were waited for; matrix products, arithmetic and copies ran while one was open for 0% of the time, Pallas kernels for 17%

profile of v5, /device:TPU:1, one launch (start us, length us, event | category | flops | bytes accessed | tf_op | source)
XLA Modules:
  0.0 98.6 jit_solution(10389535610579225926)
XLA Ops:
  0.6 3.3 %collective-permute-start = (bf16[1,1536,1024]{2,1,0:T(8,128)(2,1)}, bf16[1,1536,1024]{2,1,0:T(8,128)(2,1)S(1)}, u32[]{:S(2)}, u32[]{:S(2)}) collective-permute-start(bf16[1,1536,1024]{2,1,0:T(8,128)(2,1)} %own_latent_hbm.3), channel_id=1, source_target_pairs={{0,1},{1,0},{2,3},{3,2},{4,5},{5,4},{6,7},{7,6},{8,9},{9,8},{10,11... | collective-permute-start | bytes 9437192 | tf_op jit(solution)/shard_map/ppermute | solution.py:227
  4.0 0.0 copy-start.2
  4.0 0.0 copy-start.3
  4.0 8.5 %decode.1 = (bf16[1536,1536]{1,0:T(8,128)(2,1)}, bf16[1536,512]{1,0:T(8,128)(2,1)}, bf16[16,24,384]{2,1,0:T(8,128)(2,1)}) custom-call(bf16[1,1536,1024]{2,1,0:T(8,128)(2,1)} %own_latent_hbm.3, bf16[1024,1024]{1,0:T(8,128)(2,1)} %w_in_ref.1, bf16[96,1024]{1,0:T(8,128)(2,1)} %bitcast.1), custom_call_target="tpu_custom_call" | custom-call | tf_op jit(solution)/shard_map/decode/pallas_call | solution.py:203
  12.5 0.0 copy-start.1
  12.5 0.1 collective-permute-start.1
  12.6 21.9 %all_to_all.15.fields_ref = bf16[16,24,384]{2,1,0:T(8,128)(2,1)S(1)} all-to-all(bf16[16,24,384]{2,1,0:T(8,128)(2,1)} %get-tuple-element.18), channel_id=1, replica_groups=mesh['x'=4,'zh'=4,'y'=4,'zl'=2,'c'=2] {'x','zh'}, dimensions={0} | all-to-all | bytes 589824 | tf_op jit(solution)/shard_map/all_to_all | solution.py:225
  34.5 0.0 copy-done.2
  34.5 0.0 copy-done.3
  34.5 1.2 %pair.1 = bf16[16,24,384]{2,1,0:T(8,128)(2,1)S(1)} custom-call(bf16[16,24,384]{2,1,0:T(8,128)(2,1)S(1)} %all_to_all.15.fields_ref, bf16[96,1536]{1,0:T(8,128)(2,1)S(1)} %copy-done.2, s32[1536]{0:T(1024)S(1)} %copy-done.3), custom_call_target="tpu_custom_call" | custom-call | tf_op jit(solution)/shard_map/pair/pallas_call | solution.py:229
  35.7 15.6 %all_to_all.16.fields_ref = bf16[16,24,384]{2,1,0:T(8,128)(2,1)S(1)} all-to-all(bf16[16,24,384]{2,1,0:T(8,128)(2,1)S(1)} %pair.1), channel_id=1, replica_groups=mesh['x'=4,'zh'=4,'y'=4,'zl'=2,'c'=2] {'x','zh'}, dimensions={0} | all-to-all | bytes 589824 | tf_op jit(solution)/shard_map/all_to_all | solution.py:241
  51.3 2.3 %collective-permute-start.2 = (bf16[16,24,384]{2,1,0:T(8,128)(2,1)S(1)}, bf16[16,24,384]{2,1,0:T(8,128)(2,1)S(1)}, u32[]{:S(2)}, u32[]{:S(2)}) collective-permute-start(bf16[16,24,384]{2,1,0:T(8,128)(2,1)S(1)} %all_to_all.16.fields_ref), channel_id=1, source_target_pairs={{0,1},{1,0},{2,3},{3,2},{4,5},{5,4},{6,7},{7,6},{8,9},{9,8},{10,11... | collective-permute-start | bytes 884744 | tf_op jit(solution)/shard_map/ppermute | solution.py:242
  53.7 0.0 copy-done.1
  53.7 0.0 copy-start
  53.7 3.3 %own_grad_pre.1 = (bf16[1536,512]{1,0:T(8,128)(2,1)S(1)}, f32[128,1024]{1,0:T(8,128)S(1)}) custom-call(bf16[1536,1536]{1,0:T(8,128)(2,1)} %get-tuple-element.17.kept_hbm, bf16[16,24,384]{2,1,0:T(8,128)(2,1)S(1)} %all_to_all.16.fields_ref, bf16[96,1024]{1,0:T(8,128)(2,1)S(1)} %bitcast.2), custom_call_target="tpu_custom_call" | custom-call | flops 301989888 | bytes 6291456 | tf_op jit(solution)/shard_map/own_grad_pre/pallas_call | solution.py:245
  57.0 0.0 collective-permute-done.2.fields_ref
  57.0 0.0 collective-permute-done.1.slope_hbm
  57.0 0.0 collective-permute-done.other_latent_hbm
  57.0 0.0 copy-done
  57.0 3.5 %other_grad_pre.1 = (bf16[1536,512]{1,0:T(8,128)(2,1)S(1)}, bf16[128,640]{1,0:T(8,128)(2,1)S(1)}, bf16[128,640]{1,0:T(8,128)(2,1)S(1)}) custom-call(bf16[1536,512]{1,0:T(8,128)(2,1)S(1)} %collective-permute-done.1.slope_hbm, bf16[1,1536,1024]{2,1,0:T(8,128)(2,1)S(1)} %copy-done, bf16[1,1536,1024]{2,1,0:T(8,128)(2,1)S(1)} %collective-permute-done.other_latent_hbm, ...), custom_call_target="tpu_custom_call" | custom-call | tf_op jit(solution)/shard_map/other_grad_pre/pallas_call | solution.py:254
  60.5 0.1 collective-permute-start.3
  60.6 2.7 %collective-permute-start.4 = (bf16[128,640]{1,0:T(8,128)(2,1)S(1)}, bf16[128,640]{1,0:T(8,128)(2,1)S(1)}, u32[]{:S(2)}, u32[]{:S(2)}) collective-permute-start(bf16[128,640]{1,0:T(8,128)(2,1)S(1)} %get-tuple-element.27), channel_id=1, source_target_pairs={{0,192},{64,0},{128,64},{192,128},{1,193},{65,1},{129,65},{193,129... | collective-permute-start | bytes 491528 | tf_op jit(solution)/shard_map/ppermute | solution.py:271
  63.3 3.7 %weight_grads.1 = (f32[256,640]{1,0:T(8,128)S(1)}, f32[256,640]{1,0:T(8,128)S(1)}, f32[256,640]{1,0:T(8,128)S(1)}) custom-call(bf16[1,1536,1024]{2,1,0:T(8,128)(2,1)S(1)} %copy-done, bf16[1,1536,1024]{2,1,0:T(8,128)(2,1)S(1)} %collective-permute-done.other_latent_hbm, bf16[1536,512]{1,0:T(8,128)(2,1)S(1)} %get-tuple-element.19.own_pre, ...), custom_call_target="tpu_custom_call" | custom-call | flops 2415919104 | bytes 12582912 | tf_op jit(solution)/shard_map/weight_grads/pallas_call | solution.py:272
  67.0 0.6 collective-permute-done.3.top_ref
  67.6 0.0 collective-permute-done.4.bottom_ref
  67.6 0.1 pass_on.1
  67.7 0.1 collective-permute-start.5
  67.8 2.7 %collective-permute-start.6 = (bf16[256,640]{1,0:T(8,128)(2,1)S(1)}, bf16[256,640]{1,0:T(8,128)(2,1)S(1)}, u32[]{:S(2)}, u32[]{:S(2)}) collective-permute-start(bf16[256,640]{1,0:T(8,128)(2,1)S(1)} %get-tuple-element.29), channel_id=1, source_target_pairs={{0,192},{64,0},{128,64},{192,128},{1,193},{65,1},{129,65},{193,129... | collective-permute-start | bytes 983048 | tf_op jit(solution)/shard_map/ppermute | solution.py:288
  70.5 7.0 %collective-permute-done.5.on_ref = bf16[256,640]{1,0:T(8,128)(2,1)S(1)} collective-permute-done((bf16[256,640]{1,0:T(8,128)(2,1)S(1)}, bf16[256,640]{1,0:T(8,128)(2,1)S(1)}, u32[]{:S(2)}, u32[]{:S(2)}) %collective-permute-start.5) | collective-permute-done | bytes 327712 | tf_op jit(solution)/shard_map/ppermute | solution.py:288
  77.4 0.0 collective-permute-done.6.back_ref
  77.4 0.1 x_sum.1
  77.6 15.3 %all_to_all.17.in_ref = bf16[32,8,640]{2,1,0:T(8,128)(2,1)S(1)} all-to-all(bf16[32,8,640]{2,1,0:T(8,128)(2,1)S(1)} %x_sum.1), channel_id=1, replica_groups=mesh['x'=4,'zh'=4,'y'=4,'zl'=2,'c'=2] {'zh','y','zl'}, dimensions={0} | all-to-all | bytes 655360 | tf_op jit(solution)/shard_map/all_to_all | solution.py:292
  92.8 0.1 yz_sum.1
  92.9 4.2 %collective-permute-start.7 = (f32[4,640]{1,0:T(4,128)S(1)}, f32[4,640]{1,0:T(4,128)S(1)}, u32[]{:S(2)}, u32[]{:S(2)}) collective-permute-start(f32[4,640]{1,0:T(4,128)S(1)} %get-tuple-element.31), channel_id=1, source_target_pairs={{0,1},{1,0},{2,3},{3,2},{4,5},{5,4},{6,7},{7,6},{8,9},{9,8},{10,11... | collective-permute-start | bytes 30728 | tf_op jit(solution)/shard_map/ppermute | solution.py:295
  97.1 0.8 collective-permute-done.7.came_ref
  97.9 0.6 join.1
Async XLA Ops:
  0.6 56.4 %collective-permute-start = (bf16[1,1536,1024]{2,1,0:T(8,128)(2,1)}, bf16[1,1536,1024]{2,1,0:T(8,128)(2,1)S(1)}, u32[]{:S(2)}, u32[]{:S(2)}) collective-permute-start(bf16[1,1536,1024]{2,1,0:T(8,128)(2,1)} %own_latent_hbm.3), channel_id=1, source_target_pairs={{0,1},{1,0},{2,3},{3,2},{4,5},{5,4},{6,7},{7,6},{8,9},{9,8},{10,11... | collective-permute-start | bytes 9437192 | tf_op jit(solution)/shard_map/ppermute | solution.py:227
  4.0 30.6 %copy-start.2 = (bf16[96,1536]{1,0:T(8,128)(2,1)S(1)}, bf16[96,1536]{1,0:T(8,128)(2,1)}, u32[]{:S(2)}) copy-start(bf16[96,1536]{1,0:T(8,128)(2,1)} %target_ref.1) | copy-start | bytes 884740
  4.0 30.6 %copy-start.3 = (s32[1536]{0:T(1024)S(1)}, s32[1536]{0:T(1024)}, u32[]{:S(2)}) copy-start(s32[1536]{0:T(1024)} %mask_ref.1) | copy-start | bytes 18436
  12.5 41.2 %copy-start.1 = (bf16[1024,96]{0,1:T(8,128)(2,1)S(1)}, bf16[1024,96]{0,1:T(8,128)(2,1)}, u32[]{:S(2)}) copy-start(bf16[1024,96]{0,1:T(8,128)(2,1)} %param.7) | copy-start | bytes 589828
  12.5 44.5 %collective-permute-start.1 = (bf16[1536,512]{1,0:T(8,128)(2,1)}, bf16[1536,512]{1,0:T(8,128)(2,1)S(1)}, u32[]{:S(2)}, u32[]{:S(2)}) collective-permute-start(bf16[1536,512]{1,0:T(8,128)(2,1)} %get-tuple-element.20), channel_id=1, source_target_pairs={{0,1},{1,0},{2,3},{3,2},{4,5},{5,4},{6,7},{7,6},{8,9},{9,8},{10,11... | collective-permute-start | bytes 4718600 | tf_op jit(solution)/shard_map/ppermute | solution.py:226
  51.3 5.6 %collective-permute-start.2 = (bf16[16,24,384]{2,1,0:T(8,128)(2,1)S(1)}, bf16[16,24,384]{2,1,0:T(8,128)(2,1)S(1)}, u32[]{:S(2)}, u32[]{:S(2)}) collective-permute-start(bf16[16,24,384]{2,1,0:T(8,128)(2,1)S(1)} %all_to_all.16.fields_ref), channel_id=1, source_target_pairs={{0,1},{1,0},{2,3},{3,2},{4,5},{5,4},{6,7},{7,6},{8,9},{9,8},{10,11... | collective-permute-start | bytes 884744 | tf_op jit(solution)/shard_map/ppermute | solution.py:242
  53.7 3.3 %copy-start = (bf16[1,1536,1024]{2,1,0:T(8,128)(2,1)S(1)}, bf16[1,1536,1024]{2,1,0:T(8,128)(2,1)}, u32[]{:S(2)}) copy-start(bf16[1,1536,1024]{2,1,0:T(8,128)(2,1)} %own_latent_hbm.3) | copy-start | bytes 9437188
  60.5 7.1 %collective-permute-start.3 = (bf16[128,640]{1,0:T(8,128)(2,1)S(1)}, bf16[128,640]{1,0:T(8,128)(2,1)S(1)}, u32[]{:S(2)}, u32[]{:S(2)}) collective-permute-start(bf16[128,640]{1,0:T(8,128)(2,1)S(1)} %get-tuple-element.26), channel_id=1, source_target_pairs={{0,64},{64,128},{128,192},{192,0},{1,65},{65,129},{129,193},{193,1... | collective-permute-start | bytes 491528 | tf_op jit(solution)/shard_map/ppermute | solution.py:271
  60.6 7.0 %collective-permute-start.4 = (bf16[128,640]{1,0:T(8,128)(2,1)S(1)}, bf16[128,640]{1,0:T(8,128)(2,1)S(1)}, u32[]{:S(2)}, u32[]{:S(2)}) collective-permute-start(bf16[128,640]{1,0:T(8,128)(2,1)S(1)} %get-tuple-element.27), channel_id=1, source_target_pairs={{0,192},{64,0},{128,64},{192,128},{1,193},{65,1},{129,65},{193,129... | collective-permute-start | bytes 491528 | tf_op jit(solution)/shard_map/ppermute | solution.py:271
  67.7 9.7 %collective-permute-start.5 = (bf16[256,640]{1,0:T(8,128)(2,1)S(1)}, bf16[256,640]{1,0:T(8,128)(2,1)S(1)}, u32[]{:S(2)}, u32[]{:S(2)}) collective-permute-start(bf16[256,640]{1,0:T(8,128)(2,1)S(1)} %get-tuple-element.28), channel_id=1, source_target_pairs={{0,64},{64,128},{128,192},{192,0},{1,65},{65,129},{129,193},{193,1... | collective-permute-start | bytes 983048 | tf_op jit(solution)/shard_map/ppermute | solution.py:288
  67.8 9.6 %collective-permute-start.6 = (bf16[256,640]{1,0:T(8,128)(2,1)S(1)}, bf16[256,640]{1,0:T(8,128)(2,1)S(1)}, u32[]{:S(2)}, u32[]{:S(2)}) collective-permute-start(bf16[256,640]{1,0:T(8,128)(2,1)S(1)} %get-tuple-element.29), channel_id=1, source_target_pairs={{0,192},{64,0},{128,64},{192,128},{1,193},{65,1},{129,65},{193,129... | collective-permute-start | bytes 983048 | tf_op jit(solution)/shard_map/ppermute | solution.py:288
  92.9 5.0 %collective-permute-start.7 = (f32[4,640]{1,0:T(4,128)S(1)}, f32[4,640]{1,0:T(4,128)S(1)}, u32[]{:S(2)}, u32[]{:S(2)}) collective-permute-start(f32[4,640]{1,0:T(4,128)S(1)} %get-tuple-element.31), channel_id=1, source_target_pairs={{0,1},{1,0},{2,3},{3,2},{4,5},{5,4},{6,7},{7,6},{8,9},{9,8},{10,11... | collective-permute-start | bytes 30728 | tf_op jit(solution)/shard_map/ppermute | solution.py:295
